TPU v7x, 32 devices: a whole 2x2x4 slice. The times are simulated.
32 devices in a mesh: dp: 8 (over y, x, core), ctx: 4 (over z).
Axes of the slice: x: 2, y: 2, z: 4, core: 2. Of those that a mesh axis runs over, the one named last changes fastest.
Arguments:
- tokens_in: bfloat16 [8, 2048, 1280], P('dp', 'ctx'), may hold values from -6 to 6
- block_ids: int32 [8, 2048], P('dp'), may hold values from 0 to 15, never falling along the last dimension, each value on 1 to 256 neighbouring positions
- w_qkv: bfloat16 [1280, 3840], P('dp'), may hold values from -0.15625 to 0.15625
- w_out: bfloat16 [1280, 1280], P('dp'), may hold values from -1.25 to 1.25
- w_in: bfloat16 [1280, 1280], P('dp'), may hold values from -0.15625 to 0.15625
- w_down: bfloat16 [1280, 1280], P('dp'), may hold values from -0.15625 to 0.15625
- gain_attn: bfloat16 [1280], replicated, may hold values from 0.5 to 1.5
- gain_mlp: bfloat16 [1280], replicated, may hold values from 0.5 to 1.5
- bias_in: bfloat16 [1280], replicated, may hold values from -3 to 3
- bias_down: bfloat16 [1280], replicated, may hold values from -2 to 2
- query_scale: bfloat16 [80], replicated, may hold values from 0 to 1.5
- cotangent: bfloat16 [8, 2048, 1280], P('dp', 'ctx'), may hold values from -6 to 6
Outputs:
- output: bfloat16 [8, 2048, 1280], P('dp', 'ctx')
- grad_tokens: float32 [8, 2048, 1280], P('dp', 'ctx')
- grad_w_qkv: float32 [1280, 3840], P('dp')
- grad_w_out: float32 [1280, 1280], P('dp')
- grad_w_in: float32 [1280, 1280], P('dp')
- grad_w_down: float32 [1280, 1280], P('dp')
- grad_gain_attn: float32 [1280], replicated
- grad_gain_mlp: float32 [1280], replicated
- grad_bias_in: float32 [1280], replicated
- grad_bias_down: float32 [1280], replicated
- grad_query_scale: float32 [80], replicated
Inputs may be any that keep to these rules, and one draw needn't show every extreme that they name: `block_ids`: each sequence's block numbers never fall along positions, start at 0, take every value up to 15, and each block spans 1 to 256 positions.
All inputs are finite; a program needn't handle non-finite values.
Results may differ from a plain program's by a relative error of at most 0.02.
Values may be sent and summed in bfloat16 or wider, within the bound.
No kernel may reach another device: no remote copies, remote signals or barrier semaphores. Data moves between devices by JAX's collectives and lax.ppermute only.
A program may use at most 256 MiB of HBM per device.

v0:
```python
import math

import jax
import jax.numpy as jnp
import numpy as np
from jax import lax
from jax.sharding import PartitionSpec as P

KEY_BLOCK = 512


EPSILON = 1e-06
SOFT_FACTOR = 1.442695041
MASKED = -1e30


def dealt_blocks(block_row, groups, row_count):
    half = row_count // 2
    lower = np.arange(groups)
    sequence_order = np.stack([lower, 2 * groups - 1 - lower], 1).reshape(-1)
    stretches = block_row.reshape(2 * groups, half)
    return stretches[sequence_order].reshape(2 * groups * half)


def rms_parts(values, gain):
    inverse = lax.rsqrt(jnp.mean(values * values, -1, keepdims=True) + EPSILON)
    return (values * inverse * gain, inverse)


def rms_back(values, inverse, gain, grad_normed):
    scaled = grad_normed * gain
    normed = values * inverse
    grad_gain = jnp.sum(grad_normed * normed, 0)
    grad_values = inverse * (scaled - normed * jnp.mean(scaled * normed, -1, keepdims=True))
    return (grad_values, grad_gain)


def body(
    tokens_in,
    block_ids,
    w_qkv,
    w_out,
    w_in,
    w_down,
    gain_attn,
    gain_mlp,
    bias_in,
    bias_down,
    query_scale,
    cotangent,
):
    groups = lax.axis_size("ctx")
    place = lax.axis_index("ctx")
    row_count = tokens_in.shape[1]
    width = tokens_in.shape[2]
    head_dim = query_scale.shape[0]
    head_count = width // head_dim
    total_rows = row_count * groups
    key_block = KEY_BLOCK
    block_count = total_rows // key_block
    full_qkv, full_out, full_in, full_down = (
        lax.all_gather(w_qkv, "dp", axis=0, tiled=True),
        lax.all_gather(w_out, "dp", axis=0, tiled=True),
        lax.all_gather(w_in, "dp", axis=0, tiled=True),
        lax.all_gather(w_down, "dp", axis=0, tiled=True),
    )
    gain_one = gain_attn.astype(jnp.float32)
    gain_two = gain_mlp.astype(jnp.float32)
    key_ids = dealt_blocks(block_ids[0], groups, row_count)
    query_ids = lax.dynamic_slice_in_dim(key_ids, place * row_count, row_count)
    tokens = tokens_in[0].astype(jnp.float32)
    normed_one, inverse_one = rms_parts(tokens, gain_one)
    normed_low = normed_one.astype(jnp.bfloat16)
    qkv = jnp.dot(normed_low, full_qkv, preferred_element_type=jnp.float32)
    scale_exp = jnp.exp(query_scale.astype(jnp.float32))
    scale_dim = SOFT_FACTOR / math.sqrt(head_dim) * jnp.log1p(scale_exp)
    scale_vec = jnp.tile(scale_dim, head_count)
    query_raw = qkv[:, :width]
    query_low = (
        (query_raw * scale_vec).astype(jnp.bfloat16).reshape(row_count, head_count, head_dim)
    )
    keyval_low = qkv[:, width:].astype(jnp.bfloat16)
    keyval_all = lax.all_gather(keyval_low, "ctx", axis=0, tiled=True)

    def block_scores(start):
        block = lax.dynamic_slice_in_dim(keyval_all, start, key_block, 0)
        keys = block[:, :width].reshape(key_block, head_count, head_dim)
        values = block[:, width:].reshape(key_block, head_count, head_dim)
        block_idents = lax.dynamic_slice_in_dim(key_ids, start, key_block)
        scores = jnp.einsum("qhd,khd->hqk", query_low, keys, preferred_element_type=jnp.float32)
        allowed = block_idents[None, None, :] <= query_ids[None, :, None]
        return (jnp.where(allowed, scores, MASKED), keys, values)

    def max_step(carry, index):
        maximum, total = carry
        scores, keys, values = block_scores(index * key_block)
        new_max = jnp.maximum(maximum, jnp.max(scores, -1))
        total = total * jnp.exp(maximum - new_max) + jnp.sum(
            jnp.exp(scores - new_max[..., None]), -1
        )
        return ((new_max, total), None)

    start_max = jnp.full((head_count, row_count), MASKED, jnp.float32)
    start_total = jnp.zeros((head_count, row_count), jnp.float32)
    (maximum, total), unused = lax.scan(max_step, (start_max, start_total), jnp.arange(block_count))
    log_total = maximum + jnp.log(total)

    def out_step(accum, index):
        scores, keys, values = block_scores(index * key_block)
        probs = jnp.exp(scores - log_total[..., None]).astype(jnp.bfloat16)
        return (
            accum + jnp.einsum("hqk,khd->qhd", probs, values, preferred_element_type=jnp.float32),
            None,
        )

    start_acc = jnp.zeros((row_count, head_count, head_dim), jnp.float32)
    attended, unused = lax.scan(out_step, start_acc, jnp.arange(block_count))
    attended_low = attended.reshape(row_count, width).astype(jnp.bfloat16)
    middle = tokens + jnp.dot(attended_low, full_out, preferred_element_type=jnp.float32)
    normed_two, inverse_two = rms_parts(middle, gain_two)
    normed_two_low = normed_two.astype(jnp.bfloat16)
    hidden_pre = jnp.dot(
        normed_two_low, full_in, preferred_element_type=jnp.float32
    ) + bias_in.astype(jnp.float32)
    sigmoid_val = 1.0 / (1.0 + jnp.exp(-hidden_pre))
    hidden_low = (hidden_pre * sigmoid_val).astype(jnp.bfloat16)
    branch_two = jnp.dot(
        hidden_low, full_down, preferred_element_type=jnp.float32
    ) + bias_down.astype(jnp.float32)
    output = (middle + branch_two).astype(jnp.bfloat16)[None]
    grad_low = cotangent[0]
    grad_out = grad_low.astype(jnp.float32)
    grad_wdown = jnp.einsum("tf,td->fd", hidden_low, grad_low, preferred_element_type=jnp.float32)
    grad_bdown = jnp.sum(grad_out, 0)
    grad_hidden = jnp.einsum("td,fd->tf", grad_low, full_down, preferred_element_type=jnp.float32)
    grad_pre = (grad_hidden * sigmoid_val * (1.0 + hidden_pre * (1.0 - sigmoid_val))).astype(
        jnp.bfloat16
    )
    grad_win = jnp.einsum("td,tf->df", normed_two_low, grad_pre, preferred_element_type=jnp.float32)
    grad_bin = jnp.sum(grad_pre.astype(jnp.float32), 0)
    grad_normed_two = jnp.einsum("tf,df->td", grad_pre, full_in, preferred_element_type=jnp.float32)
    grad_mid_norm, grad_gain_two = rms_back(middle, inverse_two, gain_two, grad_normed_two)
    grad_middle = grad_out + grad_mid_norm
    grad_mid_low = grad_middle.astype(jnp.bfloat16)
    grad_wout = jnp.einsum(
        "td,te->de", attended_low, grad_mid_low, preferred_element_type=jnp.float32
    )
    grad_attended = jnp.einsum(
        "te,de->td", grad_mid_low, full_out, preferred_element_type=jnp.float32
    )
    grad_attended = grad_attended.astype(jnp.bfloat16).reshape(row_count, head_count, head_dim)
    delta = jnp.sum(grad_attended.astype(jnp.float32) * attended, -1).T

    def back_step(grad_query, index):
        scores, keys, values = block_scores(index * key_block)
        probs = jnp.exp(scores - log_total[..., None])
        probs_low = probs.astype(jnp.bfloat16)
        grad_probs = jnp.einsum(
            "qhd,khd->hqk", grad_attended, values, preferred_element_type=jnp.float32
        )
        grad_scores = (probs * (grad_probs - delta[..., None])).astype(jnp.bfloat16)
        grad_query = grad_query + jnp.einsum(
            "hqk,khd->qhd", grad_scores, keys, preferred_element_type=jnp.float32
        )
        grad_keys = jnp.einsum(
            "hqk,qhd->khd", grad_scores, query_low, preferred_element_type=jnp.float32
        )
        grad_values = jnp.einsum(
            "hqk,qhd->khd", probs_low, grad_attended, preferred_element_type=jnp.float32
        )
        joined = jnp.concatenate(
            [grad_keys.reshape(key_block, width), grad_values.reshape(key_block, width)], 1
        )
        return (grad_query, joined)

    grad_query, keyval_terms = lax.scan(back_step, start_acc, jnp.arange(block_count))
    keyval_terms = keyval_terms.reshape(total_rows, 2 * width)
    grad_keyval = lax.psum_scatter(
        keyval_terms.astype(jnp.bfloat16), "ctx", scatter_dimension=0, tiled=True
    ).astype(jnp.float32)
    grad_query_flat = grad_query.reshape(row_count, width)
    grad_qkv = jnp.concatenate([grad_query_flat * scale_vec, grad_keyval], 1).astype(jnp.bfloat16)
    scale_slope = SOFT_FACTOR / math.sqrt(head_dim) * scale_exp / (1.0 + scale_exp)
    grad_scale = (
        jnp.sum(grad_query * query_raw.reshape(row_count, head_count, head_dim), (0, 1))
        * scale_slope
    )
    grad_wqkv = jnp.einsum("td,te->de", normed_low, grad_qkv, preferred_element_type=jnp.float32)
    grad_normed_one = jnp.einsum(
        "te,de->td", grad_qkv, full_qkv, preferred_element_type=jnp.float32
    )
    grad_tok_norm, grad_gain_one = rms_back(tokens, inverse_one, gain_one, grad_normed_one)
    grad_tokens = (grad_middle + grad_tok_norm)[None]
    pieces = (
        lax.psum_scatter(
            grad_wqkv.astype(jnp.bfloat16), "dp", scatter_dimension=0, tiled=True
        ).astype(jnp.float32),
        lax.psum_scatter(
            grad_wout.astype(jnp.bfloat16), "dp", scatter_dimension=0, tiled=True
        ).astype(jnp.float32),
        lax.psum_scatter(
            grad_win.astype(jnp.bfloat16), "dp", scatter_dimension=0, tiled=True
        ).astype(jnp.float32),
        lax.psum_scatter(
            grad_wdown.astype(jnp.bfloat16), "dp", scatter_dimension=0, tiled=True
        ).astype(jnp.float32),
    )
    owned = (
        lax.psum(pieces[0].astype(jnp.bfloat16), "ctx").astype(jnp.float32),
        lax.psum(pieces[1].astype(jnp.bfloat16), "ctx").astype(jnp.float32),
        lax.psum(pieces[2].astype(jnp.bfloat16), "ctx").astype(jnp.float32),
        lax.psum(pieces[3].astype(jnp.bfloat16), "ctx").astype(jnp.float32),
    )
    small = lax.psum(
        (grad_gain_one, grad_gain_two, grad_bin, grad_bdown, grad_scale), ("dp", "ctx")
    )
    return (
        output,
        grad_tokens,
        owned[0],
        owned[1],
        owned[2],
        owned[3],
        small[0],
        small[1],
        small[2],
        small[3],
        small[4],
    )


def solution(mesh):
    return jax.shard_map(
        body,
        mesh=mesh,
        in_specs=(
            P("dp", "ctx", None),
            P("dp", None),
            P("dp", None),
            P("dp", None),
            P("dp", None),
            P("dp", None),
            P(),
            P(),
            P(),
            P(),
            P(),
            P("dp", "ctx", None),
        ),
        out_specs=(
            P("dp", "ctx", None),
            P("dp", "ctx", None),
            P("dp", None),
            P("dp", None),
            P("dp", None),
            P("dp", None),
            P(),
            P(),
            P(),
            P(),
            P(),
        ),
        check_vma=False,
    )
```

profile of v0, /device:TPU:0, one launch (start us, length us, event | category | flops | bytes accessed | tf_op | source)
XLA Modules:
  0.0 1168.1 jit_solution(16563661047465758504)
XLA Ops:
  10.3 62.8 %all-gather.6.cloned.1.call-done = bf16[1280,3840]{1,0:T(8,128)(2,1)} async-done(((bf16[160,3840]{1,0:T(8,128)(2,1)}), bf16[1280,3840]{1,0:T(8,128)(2,1)}) %all-gather.6.cloned.1.call-update) | async-done | bytes 9830416 | tf_op jit(solution)/shard_map/all_gather | solution.py:62
  73.1 8.1 fusion.44
  81.3 3.2 copy-done.14
  90.6 3.5 fusion.49
  94.8 3.0 copy.43
  97.7 172.6 %all-gather.8.cloned.1.call-done = bf16[2048,2560]{1,0:T(8,128)(2,1)} async-done(((bf16[512,2560]{1,0:T(8,128)(2,1)}), bf16[2048,2560]{1,0:T(8,128)(2,1)}) %all-gather.8.cloned.1.call-update) | async-done | bytes 10485776 | tf_op jit(solution)/shard_map/all_gather | solution.py:83
  270.3 14.5 %copy.42 = bf16[2048,2560]{0,1:T(8,128)(2,1)} copy(bf16[2048,2560]{1,0:T(8,128)(2,1)} %all-gather.8.cloned.1.call-done) | data formatting | bytes 20971520
  284.8 80.6 %while.37 = (s32[]{:T(128)}, f32[16,512]{1,0:T(8,128)S(1)}, f32[16,512]{1,0:T(8,128)S(1)}, s32[4]{0:T(128)S(1)}, s32[2048]{0:T(1024)S(1)}, /*index=5*/s32[512]{0...) while((s32[]{:T(128)}, f32[16,512]{1,0:T(8,128)S(1)}, ...), condition=%wide.region_4.5_spmd.clone, body=%wide.region_1.4_spmd.clone.sunk | while | flops 692363264 | bytes 40018120 | solution.py:105
  287.8 8.3 fusion.101
  296.1 8.8 exponential_reduce_fusion.2
  307.9 8.4 fusion.101
  316.3 8.7 exponential_reduce_fusion.2
  328.0 8.2 fusion.101
  336.2 8.7 exponential_reduce_fusion.2
  348.0 8.2 fusion.101
  356.2 9.2 exponential_reduce_fusion.2
  365.5 55.4 %while.38 = (s32[]{:T(128)}, f32[512,16,80]{0,2,1:T(8,128)}, s32[4]{0:T(128)S(1)}, bf16[2048,2560]{0,1:T(8,128)(2,1)}, s32[2048]{0:T(1024)S(1)}, /*index=5*/s32[...) while((s32[]{:T(128)}, f32[512,16,80]{0,2,1:T(8,128)}, ...), condition=%wide.region_6.7_spmd.clone, body=%wide.region_5.6_spmd.clone.sunk | while | flops 1356333056 | bytes 14983393 | solution.py:117
  367.1 3.0 constant_dynamic-slice_fusion.6
  370.1 8.9 bitcast_add_fusion.4
  383.5 9.3 bitcast_add_fusion.4
  397.3 9.3 bitcast_add_fusion.4
  408.1 3.0 constant_dynamic-slice_fusion.6
  411.1 9.3 bitcast_add_fusion.4
  420.9 3.1 convert_element_type.116
  424.0 5.8 multiply_reduce_fusion.4
  429.9 6.3 convolution_add_fusion.1
  436.1 5.8 convert_reduce_fusion.1
  454.3 186.4 %while.39 = (s32[]{:T(128)}, f32[512,16,80]{0,2,1:T(8,128)}, bf16[4,512,2560]{2,1,0:T(8,128)(2,1)}, s32[4]{0:T(128)S(1)}, bf16[2048,2560]{0,1:T(8,128)(2,1)}, /*...) while((s32[]{:T(128)}, f32[512,16,80]{0,2,1:T(8,128)}, ...), condition=%wide.region_11.12_spmd.clone, body=%wide.region_10.11_spmd.clone.sunk | while | flops 3395813376 | bytes 151101840 | solution.py:176
  459.1 8.1 fusion.117
  467.3 10.8 fusion.119
  478.0 9.3 fusion.118
  493.2 4.4 copy.74
  497.6 3.6 constant_dynamic-update-slice_fusion.2
  505.8 8.1 fusion.117
  513.9 10.8 fusion.119
  524.6 9.3 fusion.118
  539.8 4.4 copy.74
  544.2 3.5 constant_dynamic-update-slice_fusion.2
  552.3 8.1 fusion.117
  560.4 10.8 fusion.119
  571.2 9.3 fusion.118
  586.3 4.4 copy.74
  590.7 3.5 constant_dynamic-update-slice_fusion.2
  598.8 8.1 fusion.117
  606.9 10.8 fusion.119
  617.7 9.3 fusion.118
  632.8 4.4 copy.74
  637.2 3.6 constant_dynamic-update-slice_fusion.2
  642.5 5.1 convolution_convert_fusion.2
  648.9 5.4 convolution_convert_fusion.1
  656.0 4.9 convolution_convert_fusion.3
  664.8 3.0 multiply_convert_fusion
  667.8 149.8 %reduce-scatter.6.cloned.1.call-done = bf16[512,2560]{1,0:T(8,128)(2,1)} async-done(((bf16[2048,2560]{1,0:T(8,128)(2,1)}), bf16[512,2560]{1,0:T(8,128)(2,1)}) %reduce-scatter.6.cloned.1.call-update) | async-done | bytes 2621456 | tf_op jit(solution)/shard_map/reduce_scatter | solution.py:178
  817.6 10.3 convolution_convert_fusion
  828.6 3.4 copy.48
  835.8 5.4 fusion.29
  841.2 27.8 %reduce-scatter.12.cloned.1.call-done = bf16[160,1280]{1,0:T(8,128)(2,1)} async-done(((bf16[1280,1280]{1,0:T(8,128)(2,1)}), bf16[160,1280]{1,0:T(8,128)(2,1)}) %reduce-scatter.12.cloned.1.call-update) | async-done | bytes 409616 | tf_op jit(solution)/shard_map/reduce_scatter | solution.py:201
  869.0 50.3 %reduce-scatter.14.cloned.1.call-done = bf16[160,1280]{1,0:T(8,128)(2,1)} async-done(((bf16[1280,1280]{1,0:T(8,128)(2,1)}), bf16[160,1280]{1,0:T(8,128)(2,1)}) %reduce-scatter.14.cloned.1.call-update) | async-done | bytes 409616 | tf_op jit(solution)/shard_map/reduce_scatter | solution.py:204
  919.3 50.3 %reduce-scatter.10.cloned.1.call-done = bf16[160,1280]{1,0:T(8,128)(2,1)} async-done(((bf16[1280,1280]{1,0:T(8,128)(2,1)}), bf16[160,1280]{1,0:T(8,128)(2,1)}) %reduce-scatter.10.cloned.1.call-update) | async-done | bytes 409616 | tf_op jit(solution)/shard_map/reduce_scatter | solution.py:198
  969.7 81.7 %reduce-scatter.8.cloned.1.call-done = bf16[160,3840]{1,0:T(8,128)(2,1)} async-done(((bf16[1280,3840]{1,0:T(8,128)(2,1)}), bf16[160,3840]{1,0:T(8,128)(2,1)}) %reduce-scatter.8.cloned.1.call-update) | async-done | bytes 1228816 | tf_op jit(solution)/shard_map/reduce_scatter | solution.py:195
  1051.5 10.9 fusion.36
  1062.4 43.1 %all-reduce = (f32[1280]{0:T(1024)}, f32[1280]{0:T(1024)}, f32[1280]{0:T(1024)}, f32[1280]{0:T(1024)}, f32[80]{0:T(128)}) all-reduce(f32[1280]{0:T(1024)S(1)} %get-tuple-element.305, f32[1280]{0:T(1024)S(1)} %copy-done.31, f32[1280]{0:T(1024)S(1)} %copy-done.30, ...), channel_id=1, replica_groups=mesh['dp'=8,'ctx'=4] {'dp','ctx'}, use_global_device_ids=true, to_apply=%region_23.24 | all-reduce | flops 5200 | bytes 41600 | tf_op jit(solution)/shard_map/psum | solution.py:214
  1105.5 4.7 fusion.35
  1110.2 44.5 %all-reduce.4.cloned.1.call-done = (bf16[160,3840]{1,0:T(8,128)(2,1)}, bf16[160,1280]{1,0:T(8,128)(2,1)}, bf16[160,1280]{1,0:T(8,128)(2,1)}, bf16[160,1280]{1,0:T(8,128)(2,1)}) async-done(((bf16[160,3840]{1,0:T(8,128)(2,1)}, bf16[160,1280]{1,0:T(8,128)(2,1)}, bf16[160,1280]{1,0:T(8,128)(2,1)}, bf16[160,1280]{1,0:T(8,128)(2,1)}), (bf16[160,3840]{1,0:T(8,128)(2,1)}, bf16[160,1280]{1,0:T(8,128)(2,1)}, ...) | async-done | bytes 2457616 | tf_op jit(solution)/shard_map/psum | solution.py:209
  (252 shorter events, 99.6 us)
Async XLA Ops:
  7.2 65.9 %all-gather.6.cloned.1.call-start = ((), (), s32[]{:S(2)}) async-start(), calls=%async_computation.5 | async-start | bytes 11059200 | tf_op jit(solution)/shard_map/all_gather | solution.py:62
  7.9 262.4 %all-gather.8.cloned.1.call-start = ((), (), s32[]{:S(2)}) async-start(), calls=%async_computation.6 | async-start | bytes 13107200 | tf_op jit(solution)/shard_map/all_gather | solution.py:83
  8.6 72.6 %copy-start.22 = (f32[1280]{0:T(1024)}, f32[1280]{0:T(1024)S(1)}, u32[]{:S(2)}) copy-start(f32[1280]{0:T(1024)S(1)} %convert_element_type.112) | copy-start | bytes 15364
  10.3 70.9 %copy-start.27 = (f32[512]{0:T(512)}, f32[512]{0:T(512)S(1)}, u32[]{:S(2)}) copy-start(f32[512]{0:T(512)S(1)} %add_rsqrt_fusion.1) | copy-start | bytes 6148
  81.3 3.2 copy-start.14
  86.2 2.3 copy-start.39
  86.2 2.4 copy-start.37
  86.2 3.0 copy-start.29
  86.2 4.3 copy-start.34
  86.2 4.3 copy-start.35
  86.2 337.8 %all-gather.10.cloned.1.call-start = ((), (), s32[]{:S(2)}) async-start(), calls=%async_computation.7 | async-start | bytes 3686400 | tf_op jit(solution)/shard_map/all_gather | solution.py:63
  87.0 342.9 %all-gather.12.cloned.1.call-start = ((), (), s32[]{:S(2)}) async-start(), calls=%async_computation.8 | async-start | bytes 3686400 | tf_op jit(solution)/shard_map/all_gather | solution.py:64
  87.5 348.6 %all-gather.14.cloned.1.call-start = ((), (), s32[]{:S(2)}) async-start(), calls=%async_computation.9 | async-start | bytes 3686400 | tf_op jit(solution)/shard_map/all_gather | solution.py:65
  88.1 729.5 %reduce-scatter.6.cloned.1.call-start = ((), (), s32[]{:S(2)}) async-start(), calls=%async_computation.10 | async-start | bytes 13107200 | tf_op jit(solution)/shard_map/reduce_scatter | solution.py:178
  88.6 5.5 copy-start.20
  90.5 354.1 %copy-start.24 = (f32[1280]{0:T(1024)}, f32[1280]{0:T(1024)S(1)}, u32[]{:S(2)}) copy-start(f32[1280]{0:T(1024)S(1)} %convert_element_type.118) | copy-start | bytes 15364
  420.9 3.1 copy-start.4
  429.8 14.8 %copy-start.32 = (f32[512]{0:T(512)}, f32[512]{0:T(512)S(1)}, u32[]{:S(2)}) copy-start(f32[512]{0:T(512)S(1)} %add_rsqrt_fusion) | copy-start | bytes 6148
  429.8 6.3 copy-start.16
  436.1 5.8 copy-start.9
  436.1 5.8 copy-start.38
  441.9 2.6 copy-start.42
  444.6 2.9 copy-start.6
  446.1 1.5 copy-start.7
  454.5 1.4 copy-start.12
  478.0 9.3 copy-start
  488.8 2.7 copy-start.1
  488.8 2.7 copy-start.3
  497.6 3.6 copy-start.13
  524.6 9.3 copy-start
  535.5 2.7 copy-start.1
  535.5 2.7 copy-start.3
  544.2 3.5 copy-start.13
  571.2 9.3 copy-start
  582.0 2.7 copy-start.1
  582.0 2.7 copy-start.3
  590.7 3.5 copy-start.13
  617.7 9.3 copy-start
  628.5 2.7 copy-start.1
  628.5 2.7 copy-start.3
  637.2 3.6 copy-start.13
  640.8 1.7 copy-start.10
  640.8 1.7 copy-start.25
  640.8 1.7 copy-start.33
  640.8 228.2 %reduce-scatter.12.cloned.1.call-start = ((), (), s32[]{:S(2)}) async-start(), calls=%async_computation.13 | async-start | bytes 3686400 | tf_op jit(solution)/shard_map/reduce_scatter | solution.py:201
  647.6 271.7 %reduce-scatter.14.cloned.1.call-start = ((), (), s32[]{:S(2)}) async-start(), calls=%async_computation.14 | async-start | bytes 3686400 | tf_op jit(solution)/shard_map/reduce_scatter | solution.py:204
  654.3 1.7 copy-start.8
  654.3 315.3 %reduce-scatter.10.cloned.1.call-start = ((), (), s32[]{:S(2)}) async-start(), calls=%async_computation.12 | async-start | bytes 3686400 | tf_op jit(solution)/shard_map/reduce_scatter | solution.py:198
  660.9 1.7 copy-start.2
  661.0 390.4 %reduce-scatter.8.cloned.1.call-start = ((), (), s32[]{:S(2)}) async-start(), calls=%async_computation.11 | async-start | bytes 11059200 | tf_op jit(solution)/shard_map/reduce_scatter | solution.py:195
  662.7 2.1 copy-start.21
  664.8 152.9 %copy-start.23 = (f32[1280]{0:T(1024)S(1)}, f32[1280]{0:T(1024)}, u32[]{:S(2)}) copy-start(f32[1280]{0:T(1024)} %copy-done.22) | copy-start | bytes 15364
  664.8 152.9 %copy-start.28 = (f32[512]{0:T(512)S(1)}, f32[512]{0:T(512)}, u32[]{:S(2)}) copy-start(f32[512]{0:T(512)} %copy-done.27) | copy-start | bytes 6148
  827.9 326.8 %all-reduce.4.cloned.1.call-start = ((), (), s32[]{:S(2)}) async-start(), calls=%async_computation.15 | async-start | bytes 4915200 | tf_op jit(solution)/shard_map/psum | solution.py:209
  832.0 2.9 copy-start.11
  832.0 3.8 copy-start.41
  835.8 215.6 %copy-start.40 = (bf16[80]{0:T(256)(128)(2,1)S(1)}, bf16[80]{0:T(256)(128)(2,1)}, u32[]{:S(2)}) copy-start(bf16[80]{0:T(256)(128)(2,1)} %param.30) | copy-start | bytes 484
  835.8 215.6 %copy-start.5 = (bf16[1,512,1280]{2,1,0:T(8,128)(2,1)S(1)}, bf16[1,512,1280]{2,1,0:T(8,128)(2,1)}, u32[]{:S(2)}) copy-start(bf16[1,512,1280]{2,1,0:T(8,128)(2,1)} %param.20) | copy-start | bytes 3932164
  835.8 215.6 %copy-start.15 = (bf16[512,1280]{1,0:T(8,128)(2,1)S(1)}, bf16[512,1280]{1,0:T(8,128)(2,1)}, u32[]{:S(2)}) copy-start(bf16[512,1280]{1,0:T(8,128)(2,1)} %multiply_convert_fusion) | copy-start | bytes 3932164
  1051.5 10.9 copy-start.26
  1051.5 10.9 copy-start.30
  1051.5 10.9 copy-start.31
  1154.8 4.0 copy-start.19
  1154.8 5.0 copy-start.18
  (5 other events, 6.3 us)
Sparse Core Ops, SparseCore 0:
  9.9 63.1 all-gather.5
  86.3 183.9 all-gather.7
  272.2 31.0 all-gather.9
  305.0 32.8 all-gather.11
  339.6 32.8 all-gather.13
  640.9 176.6 reduce-scatter.5
  821.0 47.9 reduce-scatter.11
  872.4 46.8 reduce-scatter.13
  922.8 46.8 reduce-scatter.9
  973.1 78.2 reduce-scatter.7
  1054.0 100.7 all-reduce.3
where the time goes:
time: 1170 us
  waiting for transfers between devices  642 us (55%)
  matrix products  273 us (23%)
  local copies, waits for them, and re-layouts  110 us (9%)
  other arithmetic  74.9 us (6%)
  blocking collectives  43.1 us (4%)
  between operations  14.6 us (1%)
    all_gather x1, waiting for transfers between devices, body(): keyval_all = lax.all_gather(keyval_low, 'ctx', axis=0, tiled=True)  173 us
    reduce_scatter x1, waiting for transfers between devices, body(): lax.psum_scatter(keyval_terms.astype(jnp.bfloat16), 'ctx', scatter_dimens...  150 us
    reduce_scatter x1, waiting for transfers between devices, body(): lax.psum_scatter(grad_wqkv.astype(jnp.bfloat16), 'dp', scatter_dimension=...  81.7 us
    dot_general x8, matrix products, block_scores(): jnp.einsum('qhd,khd->hqk', query_low, keys, preferred_element_type=jnp.fl...  65.6 us
    all_gather x1, waiting for transfers between devices, body(): lax.all_gather(w_qkv, 'dp', axis=0, tiled=True)  62.8 us
    reduce_scatter x1, waiting for transfers between devices, body(): lax.psum_scatter(grad_wout.astype(jnp.bfloat16), 'dp', scatter_dimension=...  50.3 us
    reduce_scatter x1, waiting for transfers between devices, body(): lax.psum_scatter(grad_wdown.astype(jnp.bfloat16), 'dp', scatter_dimension...  50.3 us
    psum x1, waiting for transfers between devices, body(): lax.psum(pieces[0].astype(jnp.bfloat16), 'ctx').astype(jnp.float32)  44.5 us
  transfers between devices with their start and end apart: 11, of which 8 were waited for; matrix products, arithmetic and copies ran while one was open for 20% of the time, Pallas kernels for 0%

commit v1 on v0

v1 whole, which is shorter than its diff:
```python
import functools
import math

import jax
import jax.numpy as jnp
import numpy as np
from jax import lax
from jax.experimental import pallas as pl
from jax.experimental.pallas import tpu as pltpu
from jax.sharding import PartitionSpec as P

EPSILON = 1e-06
SOFT_FACTOR = 1.442695041
LOG2E = 1.4426950408889634
MASKED = -1e30
HEADS_AT_ONCE = 4
AXES = ("dp", "ctx")
BF = jnp.bfloat16
F32 = jnp.float32


def nn(a, b):
    return lax.dot_general(a, b, (((1,), (0,)), ((), ())), preferred_element_type=F32)


def nt(a, b):
    return lax.dot_general(a, b, (((1,), (1,)), ((), ())), preferred_element_type=F32)


def tile_counts(ids_ref, stretch, tile, tiles):
    low = ids_ref[stretch * tile]
    high = ids_ref[stretch * tile + tile - 1]
    full = jnp.int32(0)
    need = jnp.int32(0)
    for t in range(tiles):
        full += (ids_ref[t * tile + tile - 1] <= low).astype(jnp.int32)
        need += (ids_ref[t * tile] <= high).astype(jnp.int32)
    return full, need


def forward_kernel(
    hd, tile, ids_ref, place_ref, row_ref, col_ref, qt_ref, kt_ref, vt_ref, ot_ref, lse_ref,
    knat, acc, m_ref, l_ref,
):
    tiles = kt_ref.shape[1] // tile
    group = qt_ref.shape[0] // hd
    for h in range(group):
        knat[h] = kt_ref[h * hd : (h + 1) * hd, :].T

    def one_tile(qi, carry):
        stretch = place_ref[tiles + qi]
        full, need = tile_counts(ids_ref, stretch, tile, tiles)
        qcol = pl.ds(pl.multiple_of(qi * tile, tile), tile)
        qpos = pl.ds(pl.multiple_of(stretch * tile, tile), tile)
        m_ref[...] = jnp.full(m_ref.shape, MASKED, F32)
        l_ref[...] = jnp.zeros(l_ref.shape, F32)
        acc[...] = jnp.zeros(acc.shape, F32)

        def step(t, masked):
            off = pl.ds(pl.multiple_of(place_ref[t] * tile, tile), tile)
            if masked:
                kpos = pl.ds(pl.multiple_of(t * tile, tile), tile)
                allowed = col_ref[kpos, :] <= row_ref[:, qpos]
            scores = [
                nn(knat[h, off, :], qt_ref[h * hd : (h + 1) * hd, qcol]) for h in range(group)
            ]
            for h in range(group):
                s = scores[h]
                if masked:
                    s = jnp.where(allowed, s, MASKED)
                old = m_ref[h]
                new = jnp.maximum(old, jnp.max(s, 0, keepdims=True))
                p = jnp.exp2(s - new)
                alpha = jnp.exp2(old - new)
                l_ref[h] = l_ref[h] * alpha + jnp.sum(p, 0, keepdims=True)
                m_ref[h] = new
                acc[h] = acc[h] * alpha + nn(vt_ref[h * hd : (h + 1) * hd, off], p.astype(BF))

        def full_step(t, c):
            step(t, False)
            return c

        def mask_step(t, c):
            step(t, True)
            return c

        lax.fori_loop(0, full, full_step, 0)
        lax.fori_loop(full, need, mask_step, 0)
        for h in range(group):
            ot_ref[h * hd : (h + 1) * hd, qcol] = acc[h] / l_ref[h]
            lse_ref[h, :, qcol] = m_ref[h] + jnp.log2(l_ref[h])
        return carry

    lax.fori_loop(0, qt_ref.shape[1] // tile, one_tile, 0)


def backward_kernel(
    hd, tile, ids_ref, place_ref, row_ref, col_ref, qt_ref, kt_ref, vt_ref, dot_ref, ot_ref,
    lse_ref, dqt_ref, dkt_ref, dvt_ref, knat, vnat, dq, dk, dv, delta,
):
    tiles = kt_ref.shape[1] // tile
    group = qt_ref.shape[0] // hd
    for h in range(group):
        hs = slice(h * hd, (h + 1) * hd)
        knat[h] = kt_ref[hs, :].T
        vnat[h] = vt_ref[hs, :].T
        delta[h] = jnp.sum(dot_ref[hs, :].astype(F32) * ot_ref[hs, :], 0, keepdims=True)
    dk[...] = jnp.zeros(dk.shape, F32)
    dv[...] = jnp.zeros(dv.shape, F32)

    def one_tile(qi, carry):
        stretch = place_ref[tiles + qi]
        full, need = tile_counts(ids_ref, stretch, tile, tiles)
        qcol = pl.ds(pl.multiple_of(qi * tile, tile), tile)
        qpos = pl.ds(pl.multiple_of(stretch * tile, tile), tile)
        dq[...] = jnp.zeros(dq.shape, F32)

        def step(t, masked):
            off = pl.ds(pl.multiple_of(place_ref[t] * tile, tile), tile)
            if masked:
                kpos = pl.ds(pl.multiple_of(t * tile, tile), tile)
                allowed = col_ref[kpos, :] <= row_ref[:, qpos]
            for h in range(group):
                hs = slice(h * hd, (h + 1) * hd)
                qh, doh = qt_ref[hs, qcol], dot_ref[hs, qcol]
                s = nn(knat[h, off, :], qh)
                dp = nn(vnat[h, off, :], doh)
                if masked:
                    s = jnp.where(allowed, s, MASKED)
                p = jnp.exp2(s - lse_ref[h, :, qcol])
                ds = (p * (dp - delta[h, :, qcol])).astype(BF)
                dv[h, :, off] += nt(doh, p.astype(BF))
                dk[h, :, off] += nt(qh, ds)
                dq[h] += nn(kt_ref[hs, off], ds)

        def full_step(t, c):
            step(t, False)
            return c

        def mask_step(t, c):
            step(t, True)
            return c

        lax.fori_loop(0, full, full_step, 0)
        lax.fori_loop(full, need, mask_step, 0)
        for h in range(group):
            dqt_ref[h * hd : (h + 1) * hd, qcol] = dq[h]
        return carry

    lax.fori_loop(0, qt_ref.shape[1] // tile, one_tile, 0)
    for h in range(group):
        hs = slice(h * hd, (h + 1) * hd)
        dkt_ref[hs, :] = (dk[h] * (1.0 / LOG2E)).astype(BF)
        dvt_ref[hs, :] = dv[h].astype(BF)


def attention_specs(qt, kt, hd, group):
    nq, nk = qt.shape[1], kt.shape[1]
    small = [
        pl.BlockSpec(memory_space=pltpu.SMEM),
        pl.BlockSpec(memory_space=pltpu.SMEM),
        pl.BlockSpec((1, nk), lambda i: (0, 0)),
        pl.BlockSpec((nk, 1), lambda i: (0, 0)),
    ]
    qs = pl.BlockSpec((group * hd, nq), lambda i: (i, 0))
    ks = pl.BlockSpec((group * hd, nk), lambda i: (i, 0))
    rows = pl.BlockSpec((group, 1, nq), lambda i: (i, 0, 0))
    return small, qs, ks, rows


def attention_forward(ids, place, qt, kt, vt, hd, tile):
    heads = qt.shape[0] // hd
    nq, nk = qt.shape[1], kt.shape[1]
    group = HEADS_AT_ONCE
    small, qs, ks, rows = attention_specs(qt, kt, hd, group)
    pairs = heads * nq * nk * 0.6
    return pl.pallas_call(
        functools.partial(forward_kernel, hd, tile),
        grid=(heads // group,),
        in_specs=[*small, qs, ks, ks],
        out_specs=[qs, rows],
        out_shape=[
            jax.ShapeDtypeStruct((heads * hd, nq), F32),
            jax.ShapeDtypeStruct((heads, 1, nq), F32),
        ],
        scratch_shapes=[
            pltpu.VMEM((group, nk, hd), BF),
            pltpu.VMEM((group, hd, tile), F32),
            pltpu.VMEM((group, 1, tile), F32),
            pltpu.VMEM((group, 1, tile), F32),
        ],
        compiler_params=pltpu.CompilerParams(vmem_limit_bytes=48 << 20),
        cost_estimate=pl.CostEstimate(
            flops=int(pairs * 1024), bytes_accessed=16 << 20, transcendentals=int(pairs)
        ),
    )(ids, place, ids.reshape(1, -1), ids.reshape(-1, 1), qt, kt, vt)


def attention_backward(ids, place, qt, kt, vt, dot, ot, lse, hd, tile):
    heads = qt.shape[0] // hd
    nq, nk = qt.shape[1], kt.shape[1]
    group = HEADS_AT_ONCE
    small, qs, ks, rows = attention_specs(qt, kt, hd, group)
    pairs = heads * nq * nk * 0.6
    return pl.pallas_call(
        functools.partial(backward_kernel, hd, tile),
        grid=(heads // group,),
        in_specs=[*small, qs, ks, ks, qs, qs, rows],
        out_specs=[qs, ks, ks],
        out_shape=[
            jax.ShapeDtypeStruct((heads * hd, nq), F32),
            jax.ShapeDtypeStruct((heads * hd, nk), BF),
            jax.ShapeDtypeStruct((heads * hd, nk), BF),
        ],
        scratch_shapes=[
            pltpu.VMEM((group, nk, hd), BF),
            pltpu.VMEM((group, nk, hd), BF),
            pltpu.VMEM((group, hd, tile), F32),
            pltpu.VMEM((group, hd, nk), F32),
            pltpu.VMEM((group, hd, nk), F32),
            pltpu.VMEM((group, 1, nq), F32),
        ],
        compiler_params=pltpu.CompilerParams(vmem_limit_bytes=56 << 20),
        cost_estimate=pl.CostEstimate(
            flops=int(pairs * 2560), bytes_accessed=32 << 20, transcendentals=int(pairs)
        ),
    )(ids, place, ids.reshape(1, -1), ids.reshape(-1, 1), qt, kt, vt, dot, ot, lse)


class Plan:
    def __init__(self, dp, ctx):
        self.dp, self.ctx = dp, ctx
        self.half = ctx // 2

    def index(self, pair, core, z):
        return (pair * 2 + core) * self.ctx + z

    def perm(self, to):
        out = []
        for d in range(self.dp):
            for z in range(self.ctx):
                got = to(d // 2, d % 2, z)
                if got is not None:
                    out.append((self.index(d // 2, d % 2, z), self.index(*got)))
        return out

    def home(self, core, z):
        return core == z // self.half

    def turned(self, z, k):
        first = z // self.half * self.half
        return first + (z - first + k) % self.half

    def core_swap(self):
        return self.perm(lambda p, c, z: (p, 1 - c, z))

    def pair_swap(self, mask):
        return self.perm(lambda p, c, z: (p ^ mask, c, z))

    def z_turn(self, k):
        return self.perm(lambda p, c, z: (p, c, (z + k) % self.ctx))

    def mirror(self):
        return self.perm(
            lambda p, c, z: (p, c, z) if self.home(c, z) else (p, 1 - c, self.ctx - 1 - z)
        )

    def mirror_or_turn(self, k):
        return self.perm(
            lambda p, c, z: (p, c, self.turned(z, k))
            if self.home(c, z)
            else (p, 1 - c, self.ctx - 1 - z)
        )

    def turn(self, k, away_only):
        return self.perm(
            lambda p, c, z: None
            if away_only and self.home(c, z)
            else (p, c, self.turned(z, k))
        )

    def shard(self, core, z, k, mine):
        chip = self.turned(z, -k)
        at_home = self.home(core, z) if mine else not self.home(core, z)
        return chip if at_home else self.ctx - 1 - chip

    def places(self):
        table = np.zeros((self.dp, self.ctx, 4 * self.ctx), np.int32)
        for d in range(self.dp):
            for z in range(self.ctx):
                slots = [
                    self.shard(d % 2, z, k, mine) for k in range(self.half) for mine in (True, False)
                ]
                stretches = [s for shard in slots for s in (shard, 2 * self.ctx - 1 - shard)]
                for block, stretch in enumerate(stretches):
                    table[d, z, stretch] = block
                    table[d, z, 2 * self.ctx + block] = stretch
        return table.reshape(self.dp * self.ctx, 4 * self.ctx)


def send(value, pairs):
    return lax.ppermute(value, AXES, pairs)


def inverse_of(values):
    return lax.rsqrt(jnp.mean(values * values, -1, keepdims=True) + EPSILON)


def body(
    tokens_in, block_ids, w_qkv, w_out, w_in, w_down, gain_attn, gain_mlp, bias_in, bias_down,
    query_scale, cotangent,
):
    n = lax.axis_size("ctx")
    plan = Plan(lax.axis_size("dp"), n)
    half = plan.half
    z = lax.axis_index("ctx")
    core = lax.axis_index("dp") % 2
    pair = lax.axis_index("dp") // 2
    pairs = plan.dp // 2
    home = core == z // half
    rows = tokens_in.shape[1]
    width = tokens_in.shape[2]
    hd = query_scale.shape[0]
    heads = width // hd
    part = width // 2
    tile = rows // 2
    wrows = w_qkv.shape[0]
    core_swap = plan.core_swap()

    own = tokens_in[0]
    first = send(own, plan.mirror_or_turn(1))
    token0 = jnp.where(home, own, first)
    second = send(token0, plan.turn(1, True))
    mine = [token0, jnp.where(home, first, second)]
    for k in range(2, half):
        mine.append(send(token0, plan.turn(k, False)))
    theirs = [send(m, core_swap) for m in mine]
    x_low = jnp.concatenate([a for both in zip(mine, theirs) for a in both], 0)

    ids = jnp.where(home, block_ids[0], send(block_ids[0], core_swap))
    place = lax.dynamic_index_in_dim(
        jnp.asarray(plan.places()), lax.axis_index("dp") * n + z, 0, False
    )

    split = w_qkv.reshape(wrows, 3, 2, part)
    keep = lax.dynamic_index_in_dim(split, core, 2, False).reshape(wrows, 3 * part)
    give = lax.dynamic_index_in_dim(split, 1 - core, 2, False).reshape(wrows, 3 * part)
    got = send(give, core_swap)
    block = jnp.concatenate([jnp.where(core == 0, keep, got), jnp.where(core == 0, got, keep)], 0)
    w_half = jnp.zeros((width, 3 * part), BF)
    w_half = lax.dynamic_update_slice(w_half, block, (pair * 2 * wrows, 0))
    for mask in range(1, pairs):
        w_half = lax.dynamic_update_slice(
            w_half, send(block, plan.pair_swap(mask)), ((pair ^ mask) * 2 * wrows, 0)
        )
    full_out = lax.all_gather(w_out, "dp", axis=0, tiled=True)
    full_in = lax.all_gather(w_in, "dp", axis=0, tiled=True)
    full_down = lax.all_gather(w_down, "dp", axis=0, tiled=True)

    gain_one = gain_attn.astype(F32)
    gain_two = gain_mlp.astype(F32)
    x = x_low.astype(F32)
    inverse_one = inverse_of(x)
    normed_low = (x * inverse_one * gain_one).astype(BF)
    scale_exp = jnp.exp(query_scale.astype(F32))
    scale_dim = SOFT_FACTOR / math.sqrt(hd) * jnp.log1p(scale_exp)
    scale_vec = jnp.tile(scale_dim, heads // 2)[:, None]
    wq, wkv = w_half[:, :part], w_half[:, part:]
    raw = jnp.einsum("de,td->et", wq, normed_low[: 2 * rows], preferred_element_type=F32)
    qt = (raw * (scale_vec * LOG2E)).astype(BF)
    kvt = jnp.einsum("de,td->et", wkv, normed_low, preferred_element_type=F32).astype(BF)
    kt, vt = kvt[:part], kvt[part:]
    ot, lse = attention_forward(ids, place, qt, kt, vt, hd, tile)

    o_got = send(ot[:, rows:].astype(BF), core_swap)
    o_mine = ot[:, :rows].astype(BF)
    att = jnp.concatenate(
        [jnp.where(core == 0, o_mine, o_got), jnp.where(core == 0, o_got, o_mine)], 0
    )
    tokens = token0.astype(F32)
    grad_low = send(cotangent[0], plan.mirror())
    middle = tokens + jnp.einsum("dt,de->te", att, full_out, preferred_element_type=F32)
    inverse_two = inverse_of(middle)
    normed_two_low = (middle * inverse_two * gain_two).astype(BF)
    hidden_pre = jnp.dot(normed_two_low, full_in, preferred_element_type=F32) + bias_in.astype(F32)
    sigmoid_val = 1.0 / (1.0 + jnp.exp(-hidden_pre))
    hidden_low = (hidden_pre * sigmoid_val).astype(BF)
    branch_two = jnp.dot(hidden_low, full_down, preferred_element_type=F32) + bias_down.astype(F32)
    output = send((middle + branch_two).astype(BF), plan.mirror())

    grad_out = grad_low.astype(F32)
    grad_wdown = jnp.einsum("tf,td->fd", hidden_low, grad_low, preferred_element_type=F32)
    grad_bdown = jnp.sum(grad_out, 0)
    grad_hidden = jnp.einsum("td,fd->tf", grad_low, full_down, preferred_element_type=F32)
    grad_pre = (grad_hidden * sigmoid_val * (1.0 + hidden_pre * (1.0 - sigmoid_val))).astype(BF)
    grad_win = jnp.einsum("td,tf->df", normed_two_low, grad_pre, preferred_element_type=F32)
    grad_bin = jnp.sum(grad_pre.astype(F32), 0)
    g_two = jnp.einsum("tf,df->td", grad_pre, full_in, preferred_element_type=F32)
    u_two = g_two * gain_two
    n_two = middle * inverse_two
    grad_gain_two = jnp.sum(g_two * n_two, 0)
    grad_middle = grad_out + inverse_two * (
        u_two - n_two * jnp.mean(u_two * n_two, -1, keepdims=True)
    )
    grad_mid_low = grad_middle.astype(BF)
    grad_wout = jnp.einsum("dt,te->de", att, grad_mid_low, preferred_element_type=F32)
    grad_att = jnp.einsum("de,te->dt", full_out, grad_mid_low, preferred_element_type=F32).astype(
        BF
    )
    to_keep = lax.dynamic_slice_in_dim(grad_att, core * part, part, 0)
    to_give = lax.dynamic_slice_in_dim(grad_att, (1 - core) * part, part, 0)
    dot = jnp.concatenate([to_keep, send(to_give, core_swap)], 1)

    owned = [
        lax.psum(lax.psum_scatter(g.astype(BF), "dp", scatter_dimension=0, tiled=True), "ctx")
        for g in (grad_wout, grad_win, grad_wdown)
    ]

    dq, dkt, dvt = attention_backward(ids, place, qt, kt, vt, dot, ot, lse, hd, tile)
    grad_scale = jnp.sum((dq * qt.astype(F32)).reshape(heads // 2, hd, 2 * rows), (0, 2))
    scale_slope = SOFT_FACTOR / math.sqrt(hd) * scale_exp / (1.0 + scale_exp)
    grad_scale = grad_scale * scale_slope / (scale_dim * LOG2E)
    dqt = (dq * scale_vec).astype(BF)
    dkv = jnp.concatenate([dkt, dvt], 0)

    grad_wq = jnp.einsum("td,et->de", normed_low[: 2 * rows], dqt, preferred_element_type=F32)
    grad_wkv = jnp.einsum("td,et->de", normed_low, dkv, preferred_element_type=F32)
    grad_whalf = jnp.concatenate([grad_wq.astype(BF), grad_wkv.astype(BF)], 1)

    g_kv = jnp.einsum("et,de->td", dkv, wkv, preferred_element_type=F32)
    g_q = jnp.einsum("et,de->td", dqt, wq, preferred_element_type=F32)
    g_one = g_kv + jnp.concatenate([g_q, jnp.zeros((g_kv.shape[0] - 2 * rows, width), F32)], 0)
    n_one = x * inverse_one
    grad_gain_one = jnp.sum(g_one * n_one, 0)
    u_one = g_one * gain_one
    dx = inverse_one * (u_one - n_one * jnp.mean(u_one * n_one, -1, keepdims=True))
    slots = [dx[i * rows : (i + 1) * rows] for i in range(n)]
    slots[0] = slots[0] + grad_middle
    sums = [
        slots[2 * k] + send(slots[2 * k + 1].astype(BF), core_swap).astype(F32)
        for k in range(half)
    ]
    for k in range(2, half):
        sums[0] = sums[0] + send(sums[k].astype(BF), plan.turn(-k, False)).astype(F32)
    from_away = sums[0] + send(sums[1].astype(BF), plan.turn(-1, True)).astype(F32)
    last = send(
        jnp.where(home, sums[1], from_away).astype(BF), plan.mirror_or_turn(-1)
    ).astype(F32)
    grad_tokens = jnp.where(home, sums[0] + last, last)

    def piece(p):
        return lax.dynamic_slice_in_dim(grad_whalf, p * 2 * wrows, 2 * wrows, 0)

    total = piece(pair).astype(F32)
    for mask in range(1, pairs):
        total = total + send(piece(pair ^ mask), plan.pair_swap(mask)).astype(F32)
    total = lax.psum(total.astype(BF), "ctx")
    to_keep = lax.dynamic_slice_in_dim(total, core * wrows, wrows, 0)
    to_give = lax.dynamic_slice_in_dim(total, (1 - core) * wrows, wrows, 0)
    came = send(to_give, core_swap)
    low_part = jnp.where(core == 0, to_keep, came).reshape(wrows, 3, 1, part)
    high_part = jnp.where(core == 0, came, to_keep).reshape(wrows, 3, 1, part)
    owned_qkv = jnp.concatenate([low_part, high_part], 2).reshape(wrows, 3 * width).astype(F32)

    small = lax.psum(
        (grad_gain_one, grad_gain_two, grad_bin, grad_bdown, grad_scale), ("dp", "ctx")
    )
    return (
        output[None],
        grad_tokens[None],
        owned_qkv,
        owned[0].astype(F32),
        owned[1].astype(F32),
        owned[2].astype(F32),
        small[0],
        small[1],
        small[2],
        small[3],
        small[4],
    )


def solution(mesh):
    split = P("dp", "ctx", None)
    weight = P("dp", None)
    return jax.shard_map(
        body,
        mesh=mesh,
        in_specs=(split, weight, weight, weight, weight, weight, P(), P(), P(), P(), P(), split),
        out_specs=(split, split, weight, weight, weight, weight, P(), P(), P(), P(), P()),
        check_vma=False,
    )
```

time: 1170 us -> 637 us (0.54)
  waiting for transfers between devices: 642 us -> 125 us
  matrix products: 273 us -> 95.9 us
  Pallas kernels: 0 us -> 94.9 us
  blocking collectives: 43.1 us -> 136 us
  local copies, waits for them, and re-layouts: 110 us -> 48.7 us
  starting transfers between devices: 1.2 us -> 58.2 us
  other arithmetic: 74.9 us -> 57.8 us
    reduce_scatter x5 -> x3, waiting for transfers between devices: 360 us -> 0.01 us  [body(): lax.psum_scatter(g.astype(BF), 'dp', scatter_dimension=0, tiled=True)]
    all_gather x5 -> x3, waiting for transfers between devices: 235 us -> 0.04 us  [the longest x1 0.02 us: body(): full_in = lax.all_gather(w_in, 'dp', axis=0, tiled=True)]
    dot_general x39 -> x14, matrix products: 268 us -> 92.3 us  [the longest x1 17.8 us: body(): g_kv = jnp.einsum('et,de->td', dkv, wkv, preferred_element_type=F32)]
    ppermute x0 -> x21, waiting for transfers between devices: none -> 124 us  [send(): return lax.ppermute(value, AXES, pairs)]
    pallas_call x0 -> x2, Pallas kernels: none -> 94.9 us  [the longest x1 56.3 us: attention_backward(): pl.pallas_call(functools.partial(backward_kernel, hd, tile), grid=(heads...]
    psum x1, blocking collectives: 43.1 us -> 136 us  [body(): lax.psum((grad_gain_one, grad_gain_two, grad_bin, grad_bdown, grad_scale)...]
    ppermute x0 -> x21, starting transfers between devices: none -> 57.5 us  [send(): return lax.ppermute(value, AXES, pairs)]
    psum x1, waiting for transfers between devices: 44.5 us -> 0.01 us  [body(): total = lax.psum(total.astype(BF), 'ctx')]
  transfers between devices with their start and end apart: 11 -> 28, of which waited for: 8 -> 6; matrix products, arithmetic and copies ran while one was open for 20% -> 30% of each run, Pallas kernels for 0% -> 15%
where the time goes in v1:
time: 637 us; the launch traced here: 632 us
  blocking collectives  136 us (21%)
  waiting for transfers between devices  125 us (20%)
  matrix products  95.9 us (15%)
  Pallas kernels  94.9 us (15%)
  starting transfers between devices  58.2 us (9%)
  other arithmetic  57.8 us (9%)
  local copies, waits for them, and re-layouts  48.7 us (8%)
  between operations  15.1 us (2%)
    psum x1, blocking collectives, body(): lax.psum((grad_gain_one, grad_gain_two, grad_bin, grad_bdown, grad_scale)...  136 us
    ppermute x21, waiting for transfers between devices, send(): return lax.ppermute(value, AXES, pairs)  124 us
    ppermute x21, starting transfers between devices, send(): return lax.ppermute(value, AXES, pairs)  57.5 us
    pallas_call x1, Pallas kernels, attention_backward(): pl.pallas_call(functools.partial(backward_kernel, hd, tile), grid=(heads...  56.3 us
    pallas_call x1, Pallas kernels, attention_forward(): pl.pallas_call(functools.partial(forward_kernel, hd, tile), grid=(heads /...  38.6 us
    dot_general x1, matrix products, body(): g_kv = jnp.einsum('et,de->td', dkv, wkv, preferred_element_type=F32)  17.8 us
    dot_general x1, matrix products, body(): jnp.einsum('td,et->de', normed_low, dkv, preferred_element_type=F32)  12.9 us
    another operation x2, other arithmetic  12.8 us
  transfers between devices with their start and end apart: 28, of which 6 were waited for; matrix products, arithmetic and copies ran while one was open for 30% of the time, Pallas kernels for 15%

profile of v1, /device:TPU:0, one launch (start us, length us, event | category | flops | bytes accessed | tf_op | source)
XLA Modules:
  0.0 631.7 jit_solution(188766496139272312)
XLA Ops:
  8.7 3.1 collective-permute-start
  11.8 2.8 reshape.91
  14.6 7.9 %dynamic-slice_reduce_fusion.1 = (bf16[160,3,640]{2,1,0:T(4,128)(2,1)S(1)}, bf16[160,3,640]{2,1,0:T(4,128)(2,1)S(1)}) fusion(bf16[160,3,2,640]{3,2,1,0:T(2,128)(2,1)S(1)} %reshape.91, s32[]{:T(128)S(6)} %select_n.124, s32[]{:T(128)S(6)} %select_n.125), kind=kLoop, calls=%fused_computation.76 | loop fusion | bytes 2457608 | tf_op jit(solution)/shard_map/jit(dynamic_index_in_dim)/dynamic_slice | solution.py:346
  23.5 2.1 collective-permute-start.2
  25.6 14.2 %collective-permute-done = bf16[512,1280]{1,0:T(8,128)(2,1)S(1)} collective-permute-done((bf16[512,1280]{1,0:T(8,128)(2,1)}, bf16[512,1280]{1,0:T(8,128)(2,1)S(1)}, u32[]{:S(2)}, u32[]{:S(2)}) %collective-permute-start) | collective-permute-done | bytes 1310752 | tf_op jit(solution)/shard_map/ppermute | solution.py:302
  39.8 1.9 broadcast_select_fusion.1
  41.7 1.8 collective-permute-start.7
  43.5 3.2 collective-permute-start.1
  47.7 1.4 broadcast_select_fusion.7
  49.1 2.6 broadcast_in_dim.6
  51.7 1.6 pad_maximum_fusion.3
  53.3 1.5 collective-permute-start.3
  55.0 1.6 collective-permute-start.4
  57.0 6.4 %collective-permute-start.6 = (bf16[512,1280]{1,0:T(8,128)(2,1)S(1)}, bf16[512,1280]{1,0:T(8,128)(2,1)}, u32[]{:S(2)}, u32[]{:S(2)}) collective-permute-start(bf16[512,1280]{1,0:T(8,128)(2,1)S(1)} %broadcast_select_fusion.1), channel_id=1, source_target_pairs={{0,4},{1,5},{2,6},{3,7},{4,0},{5,1},{6,2},{7,3},{8,12},{9,13},{10,... | collective-permute-start | bytes 3932168 | tf_op jit(solution)/shard_map/ppermute | solution.py:302
  63.5 1.5 broadcast_select_fusion
  67.1 29.6 %collective-permute-done.3 = bf16[320,1920]{1,0:T(8,128)(2,1)} collective-permute-done((bf16[320,1920]{1,0:T(8,128)(2,1)}, bf16[320,1920]{1,0:T(8,128)(2,1)}, u32[]{:S(2)}, u32[]{:S(2)}) %collective-permute-start.3) | collective-permute-done | bytes 1228832 | tf_op jit(solution)/shard_map/ppermute | solution.py:302
  96.7 2.4 constant_dynamic-update-slice_fusion.4
  99.1 9.5 %collective-permute-done.4 = bf16[320,1920]{1,0:T(8,128)(2,1)} collective-permute-done((bf16[320,1920]{1,0:T(8,128)(2,1)}, bf16[320,1920]{1,0:T(8,128)(2,1)}, u32[]{:S(2)}, u32[]{:S(2)}) %collective-permute-start.4) | collective-permute-done | bytes 1228832 | tf_op jit(solution)/shard_map/ppermute | solution.py:302
  108.7 2.5 constant_dynamic-update-slice_fusion.3
  111.1 16.5 %collective-permute-done.5 = bf16[320,1920]{1,0:T(8,128)(2,1)} collective-permute-done((bf16[320,1920]{1,0:T(8,128)(2,1)}, bf16[320,1920]{1,0:T(8,128)(2,1)}, u32[]{:S(2)}, u32[]{:S(2)}) %collective-permute-start.5) | collective-permute-done | bytes 1228832 | tf_op jit(solution)/shard_map/ppermute | solution.py:302
  127.6 2.4 constant_dynamic-update-slice_fusion.2
  130.0 2.7 fusion.9
  132.8 11.4 %fusion.4 = bf16[2048,1280]{1,0:T(8,128)(2,1)S(1)} fusion(f32[1280]{0:T(1024)S(1)} %convert_element_type.130, f32[2048]{0:T(1024)S(1)} %add_rsqrt_fusion, bf16[512,1280]{1,0:T(8,128)(2,1)} %collective-permute-done.8, bf16[512,1280]{1,0:T(8,128)(2,1)S(1)} %broadcast_select_fusion, bf16[512,1280]{1,0:T(8,128)(2,1)} %collective-permute-done.6, ...), kind=kLoop, calls=%fused_computation.6 | loop fusion | flops 28835840 | bytes 10499072 | tf_op jit(solution)/shard_map/convert_element_type | solution.py:364
  144.2 9.9 %convolution_convert_fusion.3 = bf16[1280,2048]{1,0:T(8,128)(2,1)S(1)} fusion(bf16[2048,1280]{1,0:T(8,128)(2,1)S(1)} %fusion.4, bf16[1280,1920]{1,0:T(8,128)(2,1)} %constant_dynamic-update-slice_fusion.2), kind=kOutput, calls=%fused_computation.20 | convolution fusion | flops 6713507840 | bytes 13762560 | tf_op jit(solution)/shard_map/de,td->et/dot_general | solution.py:371
  154.1 3.4 multiply_convert_fusion.3.qt_ref
  157.5 3.3 fusion.42
  160.8 38.6 %shard_map.212 = (f32[640,1024]{1,0:T(8,128)S(1)}, f32[8,1,1024]{2,1,0:T(1,128)S(1)}) custom-call(s32[2048]{0:T(1024)S(1)} %broadcast_select_fusion.8.ids_ref, s32[16]{0:T(128)S(1)} %fusion.34.place_ref, s32[1,2048]{1,0:T(1,128)S(1)} %bitcast.34, s32[2048,1]{1,0:T(8,128)S(1)} %copy-done.3, bf16[640,1024]{1,0:T(8,128)(2,1)S(1)} %multiply_convert_fusion.3.qt_ref, ...), custom_call_target="tpu_custom_call" | custom-call | flops 10307921920 | bytes 16777216 | tf_op jit(solution)/shard_map/pallas_call | solution.py:177
  200.9 11.2 %collective-permute-start.11 = (bf16[512,1280]{1,0:T(8,128)(2,1)}, bf16[512,1280]{1,0:T(8,128)(2,1)}, u32[]{:S(2)}, u32[]{:S(2)}) collective-permute-start(bf16[512,1280]{1,0:T(8,128)(2,1)} %bitcast.6), channel_id=1, source_target_pairs={{0,0},{1,1},{2,5},{3,4},{4,3},{5,2},{6,6},{7,7},{8,8},{9,9},{10,13... | collective-permute-start | bytes 3932168 | tf_op jit(solution)/shard_map/ppermute | solution.py:302
  213.1 5.8 multiply_reduce_fusion.3
  219.0 4.6 convolution_add_fusion.1
  223.6 1.4 copy-done.32
  225.1 5.0 convolution_convert_fusion
  230.2 5.6 convert_reduce_fusion.1
  236.9 3.6 convolution_convert_fusion.1
  240.6 5.4 multiply_reduce_fusion.1
  246.0 2.4 convert_reduce_fusion
  248.7 1.9 convolution_convert_fusion.6
  252.2 3.6 convolution_convert_fusion.2
  256.2 2.3 pad_maximum_fusion.2.dot_ref
  258.5 56.3 %shard_map.213 = (f32[640,1024]{1,0:T(8,128)}, bf16[640,2048]{1,0:T(8,128)(2,1)}, bf16[640,2048]{1,0:T(8,128)(2,1)}) custom-call(s32[2048]{0:T(1024)} %copy-done.4, s32[16]{0:T(128)} %copy-done.5, s32[1,2048]{1,0:T(1,128)} %bitcast.35, s32[2048,1]{1,0:T(8,128)} %copy.114.col_ref, bf16[640,1024]{1,0:T(8,128)(2,1)} %copy-done.1, ...), custom_call_target="tpu_custom_call" | custom-call | flops 25769803776 | bytes 33554432 | tf_op jit(solution)/shard_map/pallas_call | solution.py:205
  314.9 7.1 %fusion.24 = f32[1024,1280]{1,0:T(8,128)} fusion(bf16[1280,1920]{1,0:T(8,128)(2,1)} %constant_dynamic-update-slice_fusion.2, f32[640,1024]{1,0:T(8,128)} %get-tuple-element.20, f32[640]{0:T(1024)S(1)} %broadcast_in_dim_tile.3), kind=kOutput, calls=%fused_computation.62 | convolution fusion | flops 1679032320 | bytes 9505280 | tf_op jit(solution)/shard_map/et,de->td/dot_general | solution.py:431
  321.9 1.9 constant_dynamic-update-slice_fusion.1
  324.7 1.9 constant_dynamic-update-slice_fusion
  326.5 17.8 %fusion.8 = (f32[1280]{0:T(1024)S(1)}, f32[2048]{0:T(1024)S(1)}, f32[2048,1280]{1,0:T(8,128)}) fusion(f32[2048]{0:T(1024)S(1)} %add_rsqrt_fusion, bf16[512,1280]{1,0:T(8,128)(2,1)} %collective-permute-done.8, bf16[512,1280]{1,0:T(8,128)(2,1)S(1)} %broadcast_select_fusion, bf16[512,1280]{1,0:T(8,128)(2,1)} %collective-permute-done.6, ...), kind=kOutput, calls=%fused_computation.10 | convolution fusion | flops 6750204928 | bytes 29517824 | tf_op jit(solution)/shard_map/et,de->td/dot_general | solution.py:430
  344.4 12.6 %fusion.39 = (bf16[2048,1280]{1,0:T(8,128)(2,1)S(1)}, f32[2048,1280]{1,0:T(8,128)S(1)}) fusion(f32[2048]{0:T(1024)S(1)} %broadcast_multiply_fusion, bf16[512,1280]{1,0:T(8,128)(2,1)} %collective-permute-done.8, bf16[512,1280]{1,0:T(8,128)(2,1)S(1)} %broadcast_select_fusion, bf16[512,1280]{1,0:T(8,128)(2,1)} %collective-permute-done.6, ...), kind=kLoop, calls=%fused_computation.109 | loop fusion | flops 36700160 | bytes 31478784 | tf_op jit(solution)/shard_map/convert.2
  357.0 1.4 fusion.41
  358.4 12.9 %convolution_convert_fusion.4 = bf16[1280,1280]{1,0:T(8,128)(2,1)S(1)} fusion(bf16[2048,1280]{1,0:T(8,128)(2,1)S(1)} %bitcast.37, bf16[1280,2048]{1,0:T(8,128)(2,1)} %constant_dynamic-update-slice_fusion), kind=kOutput, calls=%fused_computation.21 | convolution fusion | flops 6712524800 | bytes 13762560 | tf_op jit(solution)/shard_map/td,et->de/dot_general | solution.py:427
  371.4 2.4 convolution_convert_fusion.5
  375.3 2.4 collective-permute-start.19
  377.7 1.5 fusion.21
  379.2 1.9 collective-permute-start.15
  381.1 27.4 %collective-permute-done.17 = bf16[320,1920]{1,0:T(8,128)(2,1)S(1)} collective-permute-done((bf16[320,1920]{1,0:T(8,128)(2,1)S(1)}, bf16[320,1920]{1,0:T(8,128)(2,1)S(1)}, u32[]{:S(2)}, u32[]{:S(2)}) %collective-permute-start.17) | collective-permute-done | bytes 1228832 | tf_op jit(solution)/shard_map/ppermute | solution.py:302
  408.5 26.7 %collective-permute-done.18 = bf16[320,1920]{1,0:T(8,128)(2,1)S(1)} collective-permute-done((bf16[320,1920]{1,0:T(8,128)(2,1)S(1)}, bf16[320,1920]{1,0:T(8,128)(2,1)S(1)}, u32[]{:S(2)}, u32[]{:S(2)}) %collective-permute-start.18) | collective-permute-done | bytes 1228832 | tf_op jit(solution)/shard_map/ppermute | solution.py:302
  435.2 1.7 add_convert_fusion
  436.9 6.9 %fusion.12 = bf16[512,1280]{1,0:T(8,128)(2,1)} fusion(f32[512,1280]{1,0:T(8,128)} %get-tuple-element.58, bf16[1280,1280]{1,0:T(8,128)(2,1)} %all-gather.8.cloned.1.call-done, f32[1280]{0:T(1024)S(1)} %convert_element_type.139, f32[512,1280]{1,0:T(8,128)} %copy-done.32), kind=kOutput, calls=%fused_computation.36 | convolution fusion | flops 1682964480 | bytes 9835520 | tf_op jit(solution)/shard_map/dot_general | solution.py:388
  443.8 11.4 %collective-permute-start.10 = (bf16[512,1280]{1,0:T(8,128)(2,1)}, bf16[512,1280]{1,0:T(8,128)(2,1)}, u32[]{:S(2)}, u32[]{:S(2)}) collective-permute-start(bf16[512,1280]{1,0:T(8,128)(2,1)} %fusion.12), channel_id=1, source_target_pairs={{0,0},{1,1},{2,5},{3,4},{4,3},{5,2},{6,6},{7,7},{8,8},{9,9},{10,13... | collective-permute-start | bytes 3932168 | tf_op jit(solution)/shard_map/ppermute | solution.py:302
  455.2 5.1 select_convert_fusion
  460.3 9.0 %collective-permute-start.16 = (bf16[512,1280]{1,0:T(8,128)(2,1)}, bf16[512,1280]{1,0:T(8,128)(2,1)S(1)}, u32[]{:S(2)}, u32[]{:S(2)}) collective-permute-start(bf16[512,1280]{1,0:T(8,128)(2,1)} %select_convert_fusion), channel_id=1, source_target_pairs={{0,1},{1,0},{2,5},{3,4},{4,3},{5,2},{6,7},{7,6},{8,9},{9,8},{10,13... | collective-permute-start | bytes 3932168 | tf_op jit(solution)/shard_map/ppermute | solution.py:302
  469.3 2.1 multiply_reduce_fusion
  471.5 135.6 %all-reduce.1 = (f32[1280]{0:T(1024)}, f32[1280]{0:T(1024)}, f32[1280]{0:T(1024)}, f32[1280]{0:T(1024)}, f32[80]{0:T(128)}) all-reduce(f32[1280]{0:T(1024)S(1)} %get-tuple-element.21, f32[1280]{0:T(1024)S(1)} %get-tuple-element.23, f32[1280]{0:T(1024)S(1)} %get-tuple-element.61, ...), channel_id=1, replica_groups=mesh['dp'=8,'ctx'=4] {'dp','ctx'}, use_global_device_ids=true, to_apply=%region_12.13 | all-reduce | flops 5200 | bytes 41600 | tf_op jit(solution)/shard_map/psum | solution.py:465
  608.4 5.0 fusion.16
  617.2 1.9 copy.121
  619.1 3.0 reshape.96
  622.1 2.5 copy.139
  (152 shorter events, 19.6 us)
Async XLA Ops:
  7.2 206.0 %all-gather.4.cloned.1.call-start = ((), (), s32[]{:S(2)}) async-start(), calls=%async_computation.3 | async-start | bytes 3686400 | tf_op jit(solution)/shard_map/all_gather | solution.py:356
  7.9 211.1 %all-gather.6.cloned.1.call-start = ((), (), s32[]{:S(2)}) async-start(), calls=%async_computation.4 | async-start | bytes 3686400 | tf_op jit(solution)/shard_map/all_gather | solution.py:357
  8.7 221.5 %all-gather.8.cloned.1.call-start = ((), (), s32[]{:S(2)}) async-start(), calls=%async_computation.5 | async-start | bytes 3686400 | tf_op jit(solution)/shard_map/all_gather | solution.py:358
  8.7 31.1 %collective-permute-start = (bf16[512,1280]{1,0:T(8,128)(2,1)}, bf16[512,1280]{1,0:T(8,128)(2,1)S(1)}, u32[]{:S(2)}, u32[]{:S(2)}) collective-permute-start(bf16[512,1280]{1,0:T(8,128)(2,1)} %bitcast.41), channel_id=1, source_target_pairs={{0,1},{1,0},{2,5},{3,4},{4,3},{5,2},{6,7},{7,6},{8,9},{9,8},{10,13... | collective-permute-start | bytes 3932168 | tf_op jit(solution)/shard_map/ppermute | solution.py:302
  22.5 20.9 %copy-start.24 = (s32[1,2048]{1,0:T(1,128)S(1)}, s32[1,2048]{1,0:T(1,128)}, u32[]{:S(2)}) copy-start(s32[1,2048]{1,0:T(1,128)} %param.14) | copy-start | bytes 24580
  23.5 24.3 %collective-permute-start.2 = (bf16[160,1920]{1,0:T(8,128)(2,1)}, bf16[160,1920]{1,0:T(8,128)(2,1)}, u32[]{:S(2)}, u32[]{:S(2)}) collective-permute-start(bf16[160,1920]{1,0:T(8,128)(2,1)} %bitcast.13), channel_id=1, source_target_pairs={{0,4},{1,5},{2,6},{3,7},{4,0},{5,1},{6,2},{7,3},{8,12},{9,13},{10,... | collective-permute-start | bytes 1843208 | tf_op jit(solution)/shard_map/ppermute | solution.py:302
  39.8 8.0 %copy-start.11 = (bf16[512,1280]{1,0:T(8,128)(2,1)}, bf16[512,1280]{1,0:T(8,128)(2,1)S(1)}, u32[]{:S(2)}) copy-start(bf16[512,1280]{1,0:T(8,128)(2,1)S(1)} %collective-permute-done) | copy-start | bytes 3932164
  41.7 15.3 %collective-permute-start.7 = (bf16[512,1280]{1,0:T(8,128)(2,1)S(1)}, bf16[512,1280]{1,0:T(8,128)(2,1)}, u32[]{:S(2)}, u32[]{:S(2)}) collective-permute-start(bf16[512,1280]{1,0:T(8,128)(2,1)S(1)} %broadcast_select_fusion.1), channel_id=1, source_target_pairs={{2,3},{3,2},{4,5},{5,4},{10,11},{11,10},{12,13},{13,12},{18,19},{1... | collective-permute-start | bytes 3932168 | tf_op jit(solution)/shard_map/ppermute | solution.py:302
  43.5 21.4 %collective-permute-start.1 = (s32[2048]{0:T(1024)S(1)}, s32[2048]{0:T(1024)S(1)}, u32[]{:S(2)}, u32[]{:S(2)}) collective-permute-start(s32[2048]{0:T(1024)S(1)} %bitcast.42), channel_id=1, source_target_pairs={{0,4},{1,5},{2,6},{3,7},{4,0},{5,1},{6,2},{7,3},{8,12},{9,13},{10,... | collective-permute-start | bytes 24584 | tf_op jit(solution)/shard_map/ppermute | solution.py:302
  46.8 390.1 %reduce-scatter.8.cloned.1.call-start = ((), (), s32[]{:S(2)}) async-start(), calls=%async_computation.8 | async-start | bytes 3686400 | tf_op jit(solution)/shard_map/reduce_scatter | solution.py:415
  51.7 3.1 copy-start.30
  51.7 3.3 copy-start.25
  53.3 43.4 %collective-permute-start.3 = (bf16[320,1920]{1,0:T(8,128)(2,1)}, bf16[320,1920]{1,0:T(8,128)(2,1)}, u32[]{:S(2)}, u32[]{:S(2)}) collective-permute-start(bf16[320,1920]{1,0:T(8,128)(2,1)} %get-tuple-element.53), channel_id=1, source_target_pairs={{0,8},{1,9},{2,10},{3,11},{4,12},{5,13},{6,14},{7,15},{8,0},{9,1},... | collective-permute-start | bytes 3686408 | tf_op jit(solution)/shard_map/ppermute | solution.py:302
  55.0 53.6 %collective-permute-start.4 = (bf16[320,1920]{1,0:T(8,128)(2,1)}, bf16[320,1920]{1,0:T(8,128)(2,1)}, u32[]{:S(2)}, u32[]{:S(2)}) collective-permute-start(bf16[320,1920]{1,0:T(8,128)(2,1)} %get-tuple-element.53), channel_id=1, source_target_pairs={{0,16},{1,17},{2,18},{3,19},{4,20},{5,21},{6,22},{7,23},{8,24},{9,... | collective-permute-start | bytes 3686408 | tf_op jit(solution)/shard_map/ppermute | solution.py:302
  56.6 71.0 %collective-permute-start.5 = (bf16[320,1920]{1,0:T(8,128)(2,1)}, bf16[320,1920]{1,0:T(8,128)(2,1)}, u32[]{:S(2)}, u32[]{:S(2)}) collective-permute-start(bf16[320,1920]{1,0:T(8,128)(2,1)} %get-tuple-element.53), channel_id=1, source_target_pairs={{0,24},{1,25},{2,26},{3,27},{4,28},{5,29},{6,30},{7,31},{8,16},{9,... | collective-permute-start | bytes 3686408 | tf_op jit(solution)/shard_map/ppermute | solution.py:302
  57.0 73.0 %collective-permute-start.6 = (bf16[512,1280]{1,0:T(8,128)(2,1)S(1)}, bf16[512,1280]{1,0:T(8,128)(2,1)}, u32[]{:S(2)}, u32[]{:S(2)}) collective-permute-start(bf16[512,1280]{1,0:T(8,128)(2,1)S(1)} %broadcast_select_fusion.1), channel_id=1, source_target_pairs={{0,4},{1,5},{2,6},{3,7},{4,0},{5,1},{6,2},{7,3},{8,12},{9,13},{10,... | collective-permute-start | bytes 3932168 | tf_op jit(solution)/shard_map/ppermute | solution.py:302
  64.9 65.1 %collective-permute-start.8 = (bf16[512,1280]{1,0:T(8,128)(2,1)S(1)}, bf16[512,1280]{1,0:T(8,128)(2,1)}, u32[]{:S(2)}, u32[]{:S(2)}) collective-permute-start(bf16[512,1280]{1,0:T(8,128)(2,1)S(1)} %broadcast_select_fusion), channel_id=1, source_target_pairs={{0,4},{1,5},{2,6},{3,7},{4,0},{5,1},{6,2},{7,3},{8,12},{9,13},{10,... | collective-permute-start | bytes 3932168 | tf_op jit(solution)/shard_map/ppermute | solution.py:302
  65.7 95.1 %copy-start.5 = (s32[16]{0:T(128)}, s32[16]{0:T(128)S(1)}, u32[]{:S(2)}) copy-start(s32[16]{0:T(128)S(1)} %fusion.34.place_ref) | copy-start | bytes 196
  65.7 95.1 %copy-start.4 = (s32[2048]{0:T(1024)}, s32[2048]{0:T(1024)S(1)}, u32[]{:S(2)}) copy-start(s32[2048]{0:T(1024)S(1)} %broadcast_select_fusion.8.ids_ref) | copy-start | bytes 24580
  144.2 10.0 %copy-start.10 = (bf16[2048,1280]{1,0:T(8,128)(2,1)}, bf16[2048,1280]{1,0:T(8,128)(2,1)S(1)}, u32[]{:S(2)}) copy-start(bf16[2048,1280]{1,0:T(8,128)(2,1)S(1)} %fusion.4) | copy-start | bytes 15728644
  157.5 3.3 copy-start.1
  157.5 3.3 copy-start.3
  199.4 1.5 copy-start
  199.4 1.5 copy-start.6
  199.4 12.8 %copy-start.26 = (bf16[1280]{0:T(1024)(128)(2,1)S(1)}, bf16[1280]{0:T(1024)(128)(2,1)}, u32[]{:S(2)}) copy-start(bf16[1280]{0:T(1024)(128)(2,1)} %param.20) | copy-start | bytes 7684
  199.4 12.7 %copy-start.27 = (bf16[1280]{0:T(1024)(128)(2,1)S(1)}, bf16[1280]{0:T(1024)(128)(2,1)}, u32[]{:S(2)}) copy-start(bf16[1280]{0:T(1024)(128)(2,1)} %param.21) | copy-start | bytes 7684
  200.9 11.3 %collective-permute-start.9 = (bf16[640,512]{1,0:T(8,128)(2,1)S(1)}, bf16[640,512]{1,0:T(8,128)(2,1)S(1)}, u32[]{:S(2)}, u32[]{:S(2)}) collective-permute-start(bf16[640,512]{1,0:T(8,128)(2,1)S(1)} %slice.55), channel_id=1, source_target_pairs={{0,4},{1,5},{2,6},{3,7},{4,0},{5,1},{6,2},{7,3},{8,12},{9,13},{10,... | collective-permute-start | bytes 1966088 | tf_op jit(solution)/shard_map/ppermute | solution.py:302
  200.9 22.7 %collective-permute-start.11 = (bf16[512,1280]{1,0:T(8,128)(2,1)}, bf16[512,1280]{1,0:T(8,128)(2,1)}, u32[]{:S(2)}, u32[]{:S(2)}) collective-permute-start(bf16[512,1280]{1,0:T(8,128)(2,1)} %bitcast.6), channel_id=1, source_target_pairs={{0,0},{1,1},{2,5},{3,4},{4,3},{5,2},{6,6},{7,7},{8,8},{9,9},{10,13... | collective-permute-start | bytes 3932168 | tf_op jit(solution)/shard_map/ppermute | solution.py:302
  213.1 5.8 copy-start.18
  223.6 1.5 copy-start.32
  230.1 206.7 %reduce-scatter.6.cloned.1.call-start = ((), (), s32[]{:S(2)}) async-start(), calls=%async_computation.7 | async-start | bytes 3686400 | tf_op jit(solution)/shard_map/reduce_scatter | solution.py:415
  230.2 6.7 %copy-start.15 = (f32[512,1280]{1,0:T(8,128)S(1)}, f32[512,1280]{1,0:T(8,128)}, u32[]{:S(2)}) copy-start(f32[512,1280]{1,0:T(8,128)} %get-tuple-element.58) | copy-start | bytes 7864324
  235.8 1.1 copy-start.33
  240.5 196.3 %reduce-scatter.4.cloned.1.call-start = ((), (), s32[]{:S(2)}) async-start(), calls=%async_computation.6 | async-start | bytes 3686400 | tf_op jit(solution)/shard_map/reduce_scatter | solution.py:415
  240.6 5.4 copy-start.16
  246.0 2.7 copy-start.29
  248.4 3.1 copy-start.8
  250.6 1.3 copy-start.19
  250.6 1.6 copy-start.20
  251.5 4.7 collective-permute-start.12
  255.8 351.4 %all-reduce.5.cloned.1.call-start = ((), (), s32[]{:S(2)}) async-start(), calls=%async_computation.9 | async-start | bytes 4915200 | tf_op jit(solution)/shard_map/psum | solution.py:457
  314.9 7.1 %copy-start.14 = (bf16[640,2048]{1,0:T(8,128)(2,1)S(1)}, bf16[640,2048]{1,0:T(8,128)(2,1)}, u32[]{:S(2)}) copy-start(bf16[640,2048]{1,0:T(8,128)(2,1)} %get-tuple-element.18) | copy-start | bytes 7864324
  321.9 2.7 copy-start.13
  324.7 33.8 %slice-start = ((s8[5242880]{0:T(1024)(128)(4,1)}), s8[4194304]{0:T(1024)(128)(4,1)S(1)}, s32[]{:S(2)}) async-start(s8[5242880]{0:T(1024)(128)(4,1)} %bitcast.36), calls=%async_computation.10 | async-start | bytes 8388608
  326.5 31.9 %slice-start.1 = ((s8[5242880]{0:T(1024)(128)(4,1)}), s8[1048576]{0:T(1024)(128)(4,1)S(1)}, s32[]{:S(2)}) async-start(s8[5242880]{0:T(1024)(128)(4,1)} %bitcast.36), calls=%async_computation.11 | async-start | bytes 2097152
  357.0 20.7 %copy-start.7 = (f32[2048,1280]{1,0:T(8,128)}, f32[2048,1280]{1,0:T(8,128)S(1)}, u32[]{:S(2)}) copy-start(f32[2048,1280]{1,0:T(8,128)S(1)} %get-tuple-element.37) | copy-start | bytes 31457284
  358.4 13.0 %copy-start.12 = (f32[640,1024]{1,0:T(8,128)S(1)}, f32[640,1024]{1,0:T(8,128)}, u32[]{:S(2)}) copy-start(f32[640,1024]{1,0:T(8,128)} %get-tuple-element.20) | copy-start | bytes 7864324
  358.4 19.3 %collective-permute-start.14 = (bf16[512,1280]{1,0:T(8,128)(2,1)S(1)}, bf16[512,1280]{1,0:T(8,128)(2,1)S(1)}, u32[]{:S(2)}, u32[]{:S(2)}) collective-permute-start(bf16[512,1280]{1,0:T(8,128)(2,1)S(1)} %get-tuple-element.39), channel_id=1, source_target_pairs={{0,4},{1,5},{2,6},{3,7},{4,0},{5,1},{6,2},{7,3},{8,12},{9,13},{10,... | collective-permute-start | bytes 3932168 | tf_op jit(solution)/shard_map/ppermute | solution.py:302
  373.8 3.9 copy-start.28
  374.1 34.3 %collective-permute-start.17 = (bf16[320,1920]{1,0:T(8,128)(2,1)S(1)}, bf16[320,1920]{1,0:T(8,128)(2,1)S(1)}, u32[]{:S(2)}, u32[]{:S(2)}) collective-permute-start(bf16[320,1920]{1,0:T(8,128)(2,1)S(1)} %get-tuple-element.42), channel_id=1, source_target_pairs={{0,8},{1,9},{2,10},{3,11},{4,12},{5,13},{6,14},{7,15},{8,0},{9,1},... | collective-permute-start | bytes 3686408 | tf_op jit(solution)/shard_map/ppermute | solution.py:302
  374.9 60.2 %collective-permute-start.18 = (bf16[320,1920]{1,0:T(8,128)(2,1)S(1)}, bf16[320,1920]{1,0:T(8,128)(2,1)S(1)}, u32[]{:S(2)}, u32[]{:S(2)}) collective-permute-start(bf16[320,1920]{1,0:T(8,128)(2,1)S(1)} %get-tuple-element.43), channel_id=1, source_target_pairs={{0,16},{1,17},{2,18},{3,19},{4,20},{5,21},{6,22},{7,23},{8,24},{9,... | collective-permute-start | bytes 3686408 | tf_op jit(solution)/shard_map/ppermute | solution.py:302
  375.3 59.9 %collective-permute-start.19 = (bf16[320,1920]{1,0:T(8,128)(2,1)S(1)}, bf16[320,1920]{1,0:T(8,128)(2,1)S(1)}, u32[]{:S(2)}, u32[]{:S(2)}) collective-permute-start(bf16[320,1920]{1,0:T(8,128)(2,1)S(1)} %get-tuple-element.44), channel_id=1, source_target_pairs={{0,24},{1,25},{2,26},{3,27},{4,28},{5,29},{6,30},{7,31},{8,16},{9,... | collective-permute-start | bytes 3686408 | tf_op jit(solution)/shard_map/ppermute | solution.py:302
  377.7 77.5 %collective-permute-start.13 = (bf16[512,1280]{1,0:T(8,128)(2,1)}, bf16[512,1280]{1,0:T(8,128)(2,1)}, u32[]{:S(2)}, u32[]{:S(2)}) collective-permute-start(bf16[512,1280]{1,0:T(8,128)(2,1)} %get-tuple-element.38), channel_id=1, source_target_pairs={{0,4},{1,5},{2,6},{3,7},{4,0},{5,1},{6,2},{7,3},{8,12},{9,13},{10,... | collective-permute-start | bytes 3932168 | tf_op jit(solution)/shard_map/ppermute | solution.py:302
  379.2 76.1 %collective-permute-start.15 = (bf16[512,1280]{1,0:T(8,128)(2,1)}, bf16[512,1280]{1,0:T(8,128)(2,1)}, u32[]{:S(2)}, u32[]{:S(2)}) collective-permute-start(bf16[512,1280]{1,0:T(8,128)(2,1)} %fusion.21), channel_id=1, source_target_pairs={{2,3},{3,2},{4,5},{5,4},{10,11},{11,10},{12,13},{13,12},{18,19},{1... | collective-permute-start | bytes 3932168 | tf_op jit(solution)/shard_map/ppermute | solution.py:302
  436.9 18.3 %copy-start.9 = (f32[512,1280]{1,0:T(8,128)S(1)}, f32[512,1280]{1,0:T(8,128)}, u32[]{:S(2)}) copy-start(f32[512,1280]{1,0:T(8,128)} %copy-done.8) | copy-start | bytes 7864324
  443.8 25.5 %copy-start.2 = (bf16[640,1024]{1,0:T(8,128)(2,1)S(1)}, bf16[640,1024]{1,0:T(8,128)(2,1)}, u32[]{:S(2)}) copy-start(bf16[640,1024]{1,0:T(8,128)(2,1)} %copy-done.1) | copy-start | bytes 3932164
  443.8 163.3 %collective-permute-start.10 = (bf16[512,1280]{1,0:T(8,128)(2,1)}, bf16[512,1280]{1,0:T(8,128)(2,1)}, u32[]{:S(2)}, u32[]{:S(2)}) collective-permute-start(bf16[512,1280]{1,0:T(8,128)(2,1)} %fusion.12), channel_id=1, source_target_pairs={{0,0},{1,1},{2,5},{3,4},{4,3},{5,2},{6,6},{7,7},{8,8},{9,9},{10,13... | collective-permute-start | bytes 3932168 | tf_op jit(solution)/shard_map/ppermute | solution.py:302
  460.3 11.2 %copy-start.31 = (bf16[80]{0:T(256)(128)(2,1)S(1)}, bf16[80]{0:T(256)(128)(2,1)}, u32[]{:S(2)}) copy-start(bf16[80]{0:T(256)(128)(2,1)} %param.23) | copy-start | bytes 484
  460.3 148.1 %collective-permute-start.16 = (bf16[512,1280]{1,0:T(8,128)(2,1)}, bf16[512,1280]{1,0:T(8,128)(2,1)S(1)}, u32[]{:S(2)}, u32[]{:S(2)}) collective-permute-start(bf16[512,1280]{1,0:T(8,128)(2,1)} %select_convert_fusion), channel_id=1, source_target_pairs={{0,1},{1,0},{2,5},{3,4},{4,3},{5,2},{6,7},{7,6},{8,9},{9,8},{10,13... | collective-permute-start | bytes 3932168 | tf_op jit(solution)/shard_map/ppermute | solution.py:302
  608.3 5.1 copy-start.23
  608.3 6.0 copy-start.22
  608.3 7.9 %collective-permute-start.20 = (bf16[160,1920]{1,0:T(8,128)(2,1)S(1)}, bf16[160,1920]{1,0:T(8,128)(2,1)S(1)}, u32[]{:S(2)}, u32[]{:S(2)}) collective-permute-start(bf16[160,1920]{1,0:T(8,128)(2,1)S(1)} %constant_dynamic-slice_fusion), channel_id=1, source_target_pairs={{0,4},{1,5},{2,6},{3,7},{4,0},{5,1},{6,2},{7,3},{8,12},{9,13},{10,... | collective-permute-start | bytes 1843208 | tf_op jit(solution)/shard_map/ppermute | solution.py:302
  613.3 1.9 copy-start.21
  613.4 2.9 copy-start.17
Sparse Core Ops, SparseCore 0:
  9.9 35.5 all-gather.3
  47.4 46.1 all-gather.5
  95.5 50.3 all-gather.7
  230.2 57.2 reduce-scatter.7
  290.8 46.9 reduce-scatter.5
  341.0 51.3 reduce-scatter.3
  437.0 149.8 all-reduce.4

commit v2 on v1

--- a/solution.py
+++ b/solution.py
@@ -38,14 +38,28 @@
     return full, need
 
 
-def forward_kernel(
-    hd, tile, ids_ref, place_ref, row_ref, col_ref, qt_ref, kt_ref, vt_ref, ot_ref, lse_ref,
-    knat, acc, m_ref, l_ref,
-):
-    tiles = kt_ref.shape[1] // tile
+def load_keys(parts, place_ref, hd, tile, group, knat, kt=None):
+    blocks = parts[0].shape[1] // tile
+    tiles = len(parts) * blocks
+    for s, ref in enumerate(parts):
+        for b in range(blocks):
+            stretch = place_ref[tiles + s * blocks + b]
+            piece = ref[:, b * tile : (b + 1) * tile]
+            if kt is not None:
+                kt[stretch] = piece
+            if knat is not None:
+                for h in range(group):
+                    knat[h, stretch] = piece[h * hd : (h + 1) * hd, :].T
+
+
+def forward_kernel(hd, tile, n, *refs):
+    ids_ref, place_ref, row_ref, col_ref, qt_ref = refs[:5]
+    k_refs, v_refs = refs[5 : 5 + n], refs[5 + n : 5 + 2 * n]
+    ot_ref, lse_ref, knat, vt, acc, m_ref, l_ref = refs[5 + 2 * n :]
     group = qt_ref.shape[0] // hd
-    for h in range(group):
-        knat[h] = kt_ref[h * hd : (h + 1) * hd, :].T
+    tiles = vt.shape[0]
+    load_keys(k_refs, place_ref, hd, tile, group, knat)
+    load_keys(v_refs, place_ref, hd, tile, group, None, vt)
 
     def one_tile(qi, carry):
         stretch = place_ref[tiles + qi]
@@ -57,13 +71,10 @@
         acc[...] = jnp.zeros(acc.shape, F32)
 
         def step(t, masked):
-            off = pl.ds(pl.multiple_of(place_ref[t] * tile, tile), tile)
             if masked:
                 kpos = pl.ds(pl.multiple_of(t * tile, tile), tile)
                 allowed = col_ref[kpos, :] <= row_ref[:, qpos]
-            scores = [
-                nn(knat[h, off, :], qt_ref[h * hd : (h + 1) * hd, qcol]) for h in range(group)
-            ]
+            scores = [nn(knat[h, t], qt_ref[h * hd : (h + 1) * hd, qcol]) for h in range(group)]
             for h in range(group):
                 s = scores[h]
                 if masked:
@@ -74,7 +85,7 @@
                 alpha = jnp.exp2(old - new)
                 l_ref[h] = l_ref[h] * alpha + jnp.sum(p, 0, keepdims=True)
                 m_ref[h] = new
-                acc[h] = acc[h] * alpha + nn(vt_ref[h * hd : (h + 1) * hd, off], p.astype(BF))
+                acc[h] = acc[h] * alpha + nn(vt[t, h * hd : (h + 1) * hd, :], p.astype(BF))
 
         def full_step(t, c):
             step(t, False)
@@ -94,19 +105,22 @@
     lax.fori_loop(0, qt_ref.shape[1] // tile, one_tile, 0)
 
 
-def backward_kernel(
-    hd, tile, ids_ref, place_ref, row_ref, col_ref, qt_ref, kt_ref, vt_ref, dot_ref, ot_ref,
-    lse_ref, dqt_ref, dkt_ref, dvt_ref, knat, vnat, dq, dk, dv, delta,
-):
-    tiles = kt_ref.shape[1] // tile
+def backward_kernel(hd, tile, n, *refs):
+    ids_ref, place_ref, row_ref, col_ref, qt_ref = refs[:5]
+    k_refs, v_refs = refs[5 : 5 + n], refs[5 + n : 5 + 2 * n]
+    dot_ref, ot_ref, lse_ref, scale_ref = refs[5 + 2 * n : 9 + 2 * n]
+    dqt_ref, dkt_ref, dvt_ref, gs_ref = refs[9 + 2 * n : 13 + 2 * n]
+    knat, vnat, kt, dq, dk, dv, delta = refs[13 + 2 * n :]
     group = qt_ref.shape[0] // hd
+    tiles = kt.shape[0]
+    load_keys(k_refs, place_ref, hd, tile, group, knat, kt)
+    load_keys(v_refs, place_ref, hd, tile, group, vnat)
     for h in range(group):
         hs = slice(h * hd, (h + 1) * hd)
-        knat[h] = kt_ref[hs, :].T
-        vnat[h] = vt_ref[hs, :].T
         delta[h] = jnp.sum(dot_ref[hs, :].astype(F32) * ot_ref[hs, :], 0, keepdims=True)
     dk[...] = jnp.zeros(dk.shape, F32)
     dv[...] = jnp.zeros(dv.shape, F32)
+    gs_ref[...] = jnp.zeros(gs_ref.shape, F32)
 
     def one_tile(qi, carry):
         stretch = place_ref[tiles + qi]
@@ -116,22 +130,21 @@
         dq[...] = jnp.zeros(dq.shape, F32)
 
         def step(t, masked):
-            off = pl.ds(pl.multiple_of(place_ref[t] * tile, tile), tile)
             if masked:
                 kpos = pl.ds(pl.multiple_of(t * tile, tile), tile)
                 allowed = col_ref[kpos, :] <= row_ref[:, qpos]
             for h in range(group):
                 hs = slice(h * hd, (h + 1) * hd)
                 qh, doh = qt_ref[hs, qcol], dot_ref[hs, qcol]
-                s = nn(knat[h, off, :], qh)
-                dp = nn(vnat[h, off, :], doh)
+                s = nn(knat[h, t], qh)
+                dp = nn(vnat[h, t], doh)
                 if masked:
                     s = jnp.where(allowed, s, MASKED)
                 p = jnp.exp2(s - lse_ref[h, :, qcol])
                 ds = (p * (dp - delta[h, :, qcol])).astype(BF)
-                dv[h, :, off] += nt(doh, p.astype(BF))
-                dk[h, :, off] += nt(qh, ds)
-                dq[h] += nn(kt_ref[hs, off], ds)
+                dv[t, hs, :] += nt(doh, p.astype(BF))
+                dk[t, hs, :] += nt(qh, ds)
+                dq[hs, :] += nn(kt[t, hs, :], ds)
 
         def full_step(t, c):
             step(t, False)
@@ -143,88 +156,163 @@
 
         lax.fori_loop(0, full, full_step, 0)
         lax.fori_loop(full, need, mask_step, 0)
-        for h in range(group):
-            dqt_ref[h * hd : (h + 1) * hd, qcol] = dq[h]
+        gs_ref[...] += jnp.sum(dq[...] * qt_ref[:, qcol].astype(F32), 1, keepdims=True)
+        dqt_ref[:, qcol] = (dq[...] * scale_ref[...]).astype(BF)
         return carry
 
     lax.fori_loop(0, qt_ref.shape[1] // tile, one_tile, 0)
-    for h in range(group):
-        hs = slice(h * hd, (h + 1) * hd)
-        dkt_ref[hs, :] = (dk[h] * (1.0 / LOG2E)).astype(BF)
-        dvt_ref[hs, :] = dv[h].astype(BF)
-
-
-def attention_specs(qt, kt, hd, group):
-    nq, nk = qt.shape[1], kt.shape[1]
+    for b in range(tiles):
+        stretch = place_ref[tiles + b]
+        dkt_ref[:, b * tile : (b + 1) * tile] = (dk[stretch] * (1.0 / LOG2E)).astype(BF)
+        dvt_ref[:, b * tile : (b + 1) * tile] = dv[stretch].astype(BF)
+
+
+def attention_specs(qt, n, nk, hd, group):
+    nq = qt.shape[1]
+    size = group * hd
+    values = qt.shape[0] // size
     small = [
         pl.BlockSpec(memory_space=pltpu.SMEM),
         pl.BlockSpec(memory_space=pltpu.SMEM),
         pl.BlockSpec((1, nk), lambda i: (0, 0)),
         pl.BlockSpec((nk, 1), lambda i: (0, 0)),
     ]
-    qs = pl.BlockSpec((group * hd, nq), lambda i: (i, 0))
-    ks = pl.BlockSpec((group * hd, nk), lambda i: (i, 0))
+    qs = pl.BlockSpec((size, nq), lambda i: (i, 0))
+    keys = [pl.BlockSpec((size, nk // n), lambda i: (i, 0))] * n
+    vals = [pl.BlockSpec((size, nk // n), lambda i: (i + values, 0))] * n
+    ks = pl.BlockSpec((size, nk), lambda i: (i, 0))
     rows = pl.BlockSpec((group, 1, nq), lambda i: (i, 0, 0))
-    return small, qs, ks, rows
-
-
-def attention_forward(ids, place, qt, kt, vt, hd, tile):
+    return small, qs, keys, vals, ks, rows
+
+
+def attention_forward(ids, col, place, qt, kvs, hd, tile):
     heads = qt.shape[0] // hd
-    nq, nk = qt.shape[1], kt.shape[1]
+    nq, nk, n = qt.shape[1], ids.shape[0], len(kvs)
     group = HEADS_AT_ONCE
-    small, qs, ks, rows = attention_specs(qt, kt, hd, group)
+    small, qs, keys, vals, ks, rows = attention_specs(qt, n, nk, hd, group)
     pairs = heads * nq * nk * 0.6
     return pl.pallas_call(
-        functools.partial(forward_kernel, hd, tile),
+        functools.partial(forward_kernel, hd, tile, n),
         grid=(heads // group,),
-        in_specs=[*small, qs, ks, ks],
+        in_specs=[*small, qs, *keys, *vals],
         out_specs=[qs, rows],
         out_shape=[
             jax.ShapeDtypeStruct((heads * hd, nq), F32),
             jax.ShapeDtypeStruct((heads, 1, nq), F32),
         ],
         scratch_shapes=[
-            pltpu.VMEM((group, nk, hd), BF),
+            pltpu.VMEM((group, nk // tile, tile, hd), BF),
+            pltpu.VMEM((nk // tile, group * hd, tile), BF),
             pltpu.VMEM((group, hd, tile), F32),
             pltpu.VMEM((group, 1, tile), F32),
             pltpu.VMEM((group, 1, tile), F32),
         ],
-        compiler_params=pltpu.CompilerParams(vmem_limit_bytes=48 << 20),
+        compiler_params=pltpu.CompilerParams(vmem_limit_bytes=56 << 20),
         cost_estimate=pl.CostEstimate(
             flops=int(pairs * 1024), bytes_accessed=16 << 20, transcendentals=int(pairs)
         ),
-    )(ids, place, ids.reshape(1, -1), ids.reshape(-1, 1), qt, kt, vt)
-
-
-def attention_backward(ids, place, qt, kt, vt, dot, ot, lse, hd, tile):
+        name="attention_forward",
+    )(ids, place, ids.reshape(1, -1), col, qt, *kvs, *kvs)
+
+
+def attention_backward(ids, col, place, qt, kvs, dot, ot, lse, scale_vec, hd, tile):
     heads = qt.shape[0] // hd
-    nq, nk = qt.shape[1], kt.shape[1]
+    nq, nk, n = qt.shape[1], ids.shape[0], len(kvs)
     group = HEADS_AT_ONCE
-    small, qs, ks, rows = attention_specs(qt, kt, hd, group)
+    small, qs, keys, vals, ks, rows = attention_specs(qt, n, nk, hd, group)
+    one = pl.BlockSpec((group * hd, 1), lambda i: (i, 0))
     pairs = heads * nq * nk * 0.6
     return pl.pallas_call(
-        functools.partial(backward_kernel, hd, tile),
+        functools.partial(backward_kernel, hd, tile, n),
         grid=(heads // group,),
-        in_specs=[*small, qs, ks, ks, qs, qs, rows],
-        out_specs=[qs, ks, ks],
+        in_specs=[*small, qs, *keys, *vals, qs, qs, rows, one],
+        out_specs=[qs, ks, ks, one],
         out_shape=[
-            jax.ShapeDtypeStruct((heads * hd, nq), F32),
+            jax.ShapeDtypeStruct((heads * hd, nq), BF),
             jax.ShapeDtypeStruct((heads * hd, nk), BF),
             jax.ShapeDtypeStruct((heads * hd, nk), BF),
+            jax.ShapeDtypeStruct((heads * hd, 1), F32),
         ],
         scratch_shapes=[
-            pltpu.VMEM((group, nk, hd), BF),
-            pltpu.VMEM((group, nk, hd), BF),
-            pltpu.VMEM((group, hd, tile), F32),
-            pltpu.VMEM((group, hd, nk), F32),
-            pltpu.VMEM((group, hd, nk), F32),
+            pltpu.VMEM((group, nk // tile, tile, hd), BF),
+            pltpu.VMEM((group, nk // tile, tile, hd), BF),
+            pltpu.VMEM((nk // tile, group * hd, tile), BF),
+            pltpu.VMEM((group * hd, tile), F32),
+            pltpu.VMEM((nk // tile, group * hd, tile), F32),
+            pltpu.VMEM((nk // tile, group * hd, tile), F32),
             pltpu.VMEM((group, 1, nq), F32),
         ],
-        compiler_params=pltpu.CompilerParams(vmem_limit_bytes=56 << 20),
+        compiler_params=pltpu.CompilerParams(vmem_limit_bytes=60 << 20),
         cost_estimate=pl.CostEstimate(
             flops=int(pairs * 2560), bytes_accessed=32 << 20, transcendentals=int(pairs)
         ),
-    )(ids, place, ids.reshape(1, -1), ids.reshape(-1, 1), qt, kt, vt, dot, ot, lse)
+        name="attention_backward",
+    )(ids, place, ids.reshape(1, -1), col, qt, *kvs, *kvs, dot, ot, lse, scale_vec)
+
+
+def dx_kernel(part, query_tiles, dq_ref, dk_ref, dv_ref, w_ref, x_ref, gain_ref, dx_ref, gg_ref, g_ref):
+    i = pl.program_id(0)
+    width = x_ref.shape[1]
+    step = width // 5
+    dk = dk_ref[...].T
+    dv = dv_ref[...].T
+    for c in range(5):
+        cols = slice(c * step, (c + 1) * step)
+        g_ref[:, cols] = nt(dk, w_ref[cols, part : 2 * part]) + nt(dv, w_ref[cols, 2 * part :])
+
+    @pl.when(i < query_tiles)
+    def _():
+        dq = dq_ref[...].T
+        for c in range(5):
+            cols = slice(c * step, (c + 1) * step)
+            g_ref[:, cols] += nt(dq, w_ref[cols, :part])
+
+    @pl.when(i == 0)
+    def _():
+        gg_ref[...] = jnp.zeros(gg_ref.shape, F32)
+
+    x = x_ref[...].astype(F32)
+    inverse = lax.rsqrt(jnp.mean(x * x, -1, keepdims=True) + EPSILON)
+    normed = x * inverse
+    g = g_ref[...]
+    gn = g * normed
+    gg_ref[...] += jnp.sum(gn, 0, keepdims=True)
+    scaled = g * gain_ref[...]
+    mean = jnp.mean(gn * gain_ref[...], -1, keepdims=True)
+    dx_ref[...] = (inverse * (scaled - normed * mean)).astype(BF)
+
+
+def input_gradient(dqt, dkt, dvt, w_half, x_low, gain):
+    part, nq = dqt.shape
+    nk, width = x_low.shape
+    tile = 256
+    query_tiles = nq // tile
+    return pl.pallas_call(
+        functools.partial(dx_kernel, part, query_tiles),
+        grid=(nk // tile,),
+        in_specs=[
+            pl.BlockSpec((part, tile), lambda i: (0, jnp.minimum(i, query_tiles - 1))),
+            pl.BlockSpec((part, tile), lambda i: (0, i)),
+            pl.BlockSpec((part, tile), lambda i: (0, i)),
+            pl.BlockSpec((width, 3 * part), lambda i: (0, 0)),
+            pl.BlockSpec((tile, width), lambda i: (i, 0)),
+            pl.BlockSpec((1, width), lambda i: (0, 0)),
+        ],
+        out_specs=[
+            pl.BlockSpec((tile, width), lambda i: (i, 0)),
+            pl.BlockSpec((1, width), lambda i: (0, 0)),
+        ],
+        out_shape=[
+            jax.ShapeDtypeStruct((nk, width), BF),
+            jax.ShapeDtypeStruct((1, width), F32),
+        ],
+        scratch_shapes=[pltpu.VMEM((tile, width), F32)],
+        compiler_params=pltpu.CompilerParams(vmem_limit_bytes=40 << 20),
+        cost_estimate=pl.CostEstimate(
+            flops=2 * width * part * (2 * nk + nq), bytes_accessed=24 << 20, transcendentals=0
+        ),
+        name="input_gradient",
+    )(dqt, dkt, dvt, w_half, x_low, gain)
 
 
 class Plan:
@@ -259,6 +347,20 @@
 
     def z_turn(self, k):
         return self.perm(lambda p, c, z: (p, c, (z + k) % self.ctx))
+
+    def line_in(self, s):
+        last = self.ctx - 1
+        to = {s: s + 1, last - s: last - s - 1}
+        return self.perm(lambda p, c, z: (p, c, to[z]) if z in to else None)
+
+    def line_out(self, s):
+        last = self.ctx - 1
+        to = {s + 1: s, last - s - 1: last - s}
+        return self.perm(lambda p, c, z: (p, c, to[z]) if z in to else None)
+
+    def line_middle(self):
+        to = {self.half - 1: self.half, self.half: self.half - 1}
+        return self.perm(lambda p, c, z: (p, c, to[z]) if z in to else None)
 
     def mirror(self):
         return self.perm(
@@ -300,6 +402,18 @@
 
 def send(value, pairs):
     return lax.ppermute(value, AXES, pairs)
+
+
+def line_sum(value, plan, z, kind):
+    total = value.astype(F32)
+    for s in range(plan.half - 1):
+        total = total + send(total.astype(kind), plan.line_in(s)).astype(F32)
+    sent = total.astype(kind)
+    total = (sent.astype(F32) + send(sent, plan.line_middle()).astype(F32)).astype(kind)
+    for s in reversed(range(plan.half - 1)):
+        back = send(total, plan.line_out(s))
+        total = jnp.where((z == s) | (z == plan.ctx - 1 - s), back, total)
+    return total
 
 
 def inverse_of(values):
@@ -327,6 +441,24 @@
     wrows = w_qkv.shape[0]
     core_swap = plan.core_swap()
 
+    def columns(which):
+        return jnp.concatenate(
+            [
+                lax.dynamic_slice(w_qkv, (0, i * width + which * part), (wrows, part))
+                for i in range(3)
+            ],
+            1,
+        )
+
+    got = send(columns(1 - core), core_swap)
+    keep = columns(core)
+    block = jnp.concatenate([jnp.where(core == 0, keep, got), jnp.where(core == 0, got, keep)], 0)
+    arrived = [send(block, plan.pair_swap(mask)) for mask in range(1, pairs)]
+    w_half = jnp.zeros((width, 3 * part), BF)
+    w_half = lax.dynamic_update_slice(w_half, block, (pair * 2 * wrows, 0))
+    for mask, piece in enumerate(arrived, 1):
+        w_half = lax.dynamic_update_slice(w_half, piece, ((pair ^ mask) * 2 * wrows, 0))
+
     own = tokens_in[0]
     first = send(own, plan.mirror_or_turn(1))
     token0 = jnp.where(home, own, first)
@@ -335,42 +467,40 @@
     for k in range(2, half):
         mine.append(send(token0, plan.turn(k, False)))
     theirs = [send(m, core_swap) for m in mine]
-    x_low = jnp.concatenate([a for both in zip(mine, theirs) for a in both], 0)
+    slots = [a for both in zip(mine, theirs) for a in both]
+    x_low = jnp.concatenate(slots, 0)
 
     ids = jnp.where(home, block_ids[0], send(block_ids[0], core_swap))
     place = lax.dynamic_index_in_dim(
         jnp.asarray(plan.places()), lax.axis_index("dp") * n + z, 0, False
     )
-
-    split = w_qkv.reshape(wrows, 3, 2, part)
-    keep = lax.dynamic_index_in_dim(split, core, 2, False).reshape(wrows, 3 * part)
-    give = lax.dynamic_index_in_dim(split, 1 - core, 2, False).reshape(wrows, 3 * part)
-    got = send(give, core_swap)
-    block = jnp.concatenate([jnp.where(core == 0, keep, got), jnp.where(core == 0, got, keep)], 0)
-    w_half = jnp.zeros((width, 3 * part), BF)
-    w_half = lax.dynamic_update_slice(w_half, block, (pair * 2 * wrows, 0))
-    for mask in range(1, pairs):
-        w_half = lax.dynamic_update_slice(
-            w_half, send(block, plan.pair_swap(mask)), ((pair ^ mask) * 2 * wrows, 0)
-        )
-    full_out = lax.all_gather(w_out, "dp", axis=0, tiled=True)
-    full_in = lax.all_gather(w_in, "dp", axis=0, tiled=True)
-    full_down = lax.all_gather(w_down, "dp", axis=0, tiled=True)
+    col = ids.reshape(-1, 1)
+
+    late_out, late_in, late_down, w_half = lax.optimization_barrier((w_out, w_in, w_down, w_half))
+    full_out = lax.all_gather(late_out, "dp", axis=0, tiled=True)
+    full_in = lax.all_gather(late_in, "dp", axis=0, tiled=True)
+    full_down = lax.all_gather(late_down, "dp", axis=0, tiled=True)
 
     gain_one = gain_attn.astype(F32)
     gain_two = gain_mlp.astype(F32)
-    x = x_low.astype(F32)
-    inverse_one = inverse_of(x)
-    normed_low = (x * inverse_one * gain_one).astype(BF)
     scale_exp = jnp.exp(query_scale.astype(F32))
     scale_dim = SOFT_FACTOR / math.sqrt(hd) * jnp.log1p(scale_exp)
     scale_vec = jnp.tile(scale_dim, heads // 2)[:, None]
     wq, wkv = w_half[:, :part], w_half[:, part:]
+
+    def normed(values):
+        v = values.astype(F32)
+        return (v * inverse_of(v) * gain_one).astype(BF)
+
+    normed_slots = [normed(s) for s in slots]
+    kvs = [
+        jnp.einsum("de,td->et", wkv, s, preferred_element_type=F32).astype(BF)
+        for s in normed_slots
+    ]
+    normed_low = jnp.concatenate(normed_slots, 0)
     raw = jnp.einsum("de,td->et", wq, normed_low[: 2 * rows], preferred_element_type=F32)
     qt = (raw * (scale_vec * LOG2E)).astype(BF)
-    kvt = jnp.einsum("de,td->et", wkv, normed_low, preferred_element_type=F32).astype(BF)
-    kt, vt = kvt[:part], kvt[part:]
-    ot, lse = attention_forward(ids, place, qt, kt, vt, hd, tile)
+    ot, lse = attention_forward(ids, col, place, qt, kvs, hd, tile)
 
     o_got = send(ot[:, rows:].astype(BF), core_swap)
     o_mine = ot[:, :rows].astype(BF)
@@ -411,35 +541,35 @@
     to_give = lax.dynamic_slice_in_dim(grad_att, (1 - core) * part, part, 0)
     dot = jnp.concatenate([to_keep, send(to_give, core_swap)], 1)
 
-    owned = [
-        lax.psum(lax.psum_scatter(g.astype(BF), "dp", scatter_dimension=0, tiled=True), "ctx")
-        for g in (grad_wout, grad_win, grad_wdown)
-    ]
-
-    dq, dkt, dvt = attention_backward(ids, place, qt, kt, vt, dot, ot, lse, hd, tile)
-    grad_scale = jnp.sum((dq * qt.astype(F32)).reshape(heads // 2, hd, 2 * rows), (0, 2))
+    joined = jnp.concatenate([g.astype(BF) for g in (grad_wdown, grad_win, grad_wout)], 1)
+    scattered = lax.psum_scatter(joined, "dp", scatter_dimension=0, tiled=True)
+
+    dqt, dkt, dvt, gs = attention_backward(
+        ids, col, place, qt, kvs, dot, ot, lse, scale_vec, hd, tile
+    )
+    grad_scale = jnp.sum(gs.reshape(heads // 2, hd), 0)
     scale_slope = SOFT_FACTOR / math.sqrt(hd) * scale_exp / (1.0 + scale_exp)
     grad_scale = grad_scale * scale_slope / (scale_dim * LOG2E)
-    dqt = (dq * scale_vec).astype(BF)
-    dkv = jnp.concatenate([dkt, dvt], 0)
-
-    grad_wq = jnp.einsum("td,et->de", normed_low[: 2 * rows], dqt, preferred_element_type=F32)
-    grad_wkv = jnp.einsum("td,et->de", normed_low, dkv, preferred_element_type=F32)
-    grad_whalf = jnp.concatenate([grad_wq.astype(BF), grad_wkv.astype(BF)], 1)
-
-    g_kv = jnp.einsum("et,de->td", dkv, wkv, preferred_element_type=F32)
-    g_q = jnp.einsum("et,de->td", dqt, wq, preferred_element_type=F32)
-    g_one = g_kv + jnp.concatenate([g_q, jnp.zeros((g_kv.shape[0] - 2 * rows, width), F32)], 0)
-    n_one = x * inverse_one
-    grad_gain_one = jnp.sum(g_one * n_one, 0)
-    u_one = g_one * gain_one
-    dx = inverse_one * (u_one - n_one * jnp.mean(u_one * n_one, -1, keepdims=True))
-    slots = [dx[i * rows : (i + 1) * rows] for i in range(n)]
-    slots[0] = slots[0] + grad_middle
+
+    query_rows = normed_low[: 2 * rows]
+    grads = [
+        jnp.einsum("td,et->de", a, g, preferred_element_type=F32).astype(BF)
+        for a, g in ((query_rows, dqt), (normed_low, dkt), (normed_low, dvt))
+    ]
+    grad_whalf = jnp.concatenate(grads, 1)
+
+    def piece_of(p):
+        return lax.dynamic_slice_in_dim(grad_whalf, p * 2 * wrows, 2 * wrows, 0)
+
+    pieces = [send(piece_of(pair ^ mask), plan.pair_swap(mask)) for mask in range(1, pairs)]
+
+    dx, grad_gain_one = input_gradient(dqt, dkt, dvt, w_half, x_low, gain_one.reshape(1, -1))
+    parts = [dx[i * rows : (i + 1) * rows] for i in range(n)]
     sums = [
-        slots[2 * k] + send(slots[2 * k + 1].astype(BF), core_swap).astype(F32)
+        parts[2 * k].astype(F32) + send(parts[2 * k + 1], core_swap).astype(F32)
         for k in range(half)
     ]
+    sums[0] = sums[0] + grad_middle
     for k in range(2, half):
         sums[0] = sums[0] + send(sums[k].astype(BF), plan.turn(-k, False)).astype(F32)
     from_away = sums[0] + send(sums[1].astype(BF), plan.turn(-1, True)).astype(F32)
@@ -448,35 +578,46 @@
     ).astype(F32)
     grad_tokens = jnp.where(home, sums[0] + last, last)
 
-    def piece(p):
-        return lax.dynamic_slice_in_dim(grad_whalf, p * 2 * wrows, 2 * wrows, 0)
-
-    total = piece(pair).astype(F32)
-    for mask in range(1, pairs):
-        total = total + send(piece(pair ^ mask), plan.pair_swap(mask)).astype(F32)
-    total = lax.psum(total.astype(BF), "ctx")
-    to_keep = lax.dynamic_slice_in_dim(total, core * wrows, wrows, 0)
-    to_give = lax.dynamic_slice_in_dim(total, (1 - core) * wrows, wrows, 0)
-    came = send(to_give, core_swap)
-    low_part = jnp.where(core == 0, to_keep, came).reshape(wrows, 3, 1, part)
-    high_part = jnp.where(core == 0, came, to_keep).reshape(wrows, 3, 1, part)
-    owned_qkv = jnp.concatenate([low_part, high_part], 2).reshape(wrows, 3 * width).astype(F32)
-
-    small = lax.psum(
-        (grad_gain_one, grad_gain_two, grad_bin, grad_bdown, grad_scale), ("dp", "ctx")
-    )
+    total = piece_of(pair).astype(F32)
+    for piece in pieces:
+        total = total + piece.astype(F32)
+    others = [
+        line_sum(scattered[:, i * width : (i + 1) * width], plan, z, BF).astype(F32)
+        for i in range(3)
+    ]
+    swapped = []
+    for i in range(3):
+        one = line_sum(total[:, i * part : (i + 1) * part], plan, z, BF)
+        to_keep = lax.dynamic_slice_in_dim(one, core * wrows, wrows, 0)
+        to_give = lax.dynamic_slice_in_dim(one, (1 - core) * wrows, wrows, 0)
+        came = send(to_give, core_swap)
+        swapped.append(jnp.where(core == 0, to_keep, came))
+        swapped.append(jnp.where(core == 0, came, to_keep))
+    owned_qkv = jnp.concatenate(swapped, 1).astype(F32)
+
+    small = jnp.concatenate(
+        [grad_gain_one.reshape(-1), grad_gain_two, grad_bin, grad_bdown, grad_scale]
+    )
+    small_size = small.shape[0]
+    small = jnp.pad(small, (0, -small_size % 1024)).reshape(-1, 128)
+    small = small + send(small, core_swap)
+    mask = 1
+    while mask < pairs:
+        small = small + send(small, plan.pair_swap(mask))
+        mask *= 2
+    small = line_sum(small, plan, z, F32).reshape(-1)
     return (
         output[None],
         grad_tokens[None],
         owned_qkv,
-        owned[0].astype(F32),
-        owned[1].astype(F32),
-        owned[2].astype(F32),
-        small[0],
-        small[1],
-        small[2],
-        small[3],
-        small[4],
+        others[2],
+        others[1],
+        others[0],
+        small[:width],
+        small[width : 2 * width],
+        small[2 * width : 3 * width],
+        small[3 * width : 4 * width],
+        small[4 * width : small_size],
     )
 
 

time: 637 us -> 669 us (1.050)
  blocking collectives: 136 us -> 0 us
  waiting for transfers between devices: 125 us -> 210 us
  starting transfers between devices: 58.2 us -> 116 us
  local copies, waits for them, and re-layouts: 48.7 us -> 91 us
  matrix products: 95.9 us -> 73.1 us
  Pallas kernels: 94.9 us -> 109 us
  other arithmetic: 57.8 us -> 47.5 us
    psum x1 -> x0, blocking collectives: 136 us -> none  [body(): lax.psum((grad_gain_one, grad_gain_two, grad_bin, grad_bdown, grad_scale)...]
    ppermute x21 -> x47, waiting for transfers between devices: 124 us -> 209 us  [send(): return lax.ppermute(value, AXES, pairs)]
    ppermute x21 -> x47, starting transfers between devices: 57.5 us -> 115 us  [send(): return lax.ppermute(value, AXES, pairs)]
    unnamed x76 -> x93, local copies, waits for them, and re-layouts: 11.7 us -> 36.3 us
    ppermute x0 -> x12, local copies, waits for them, and re-layouts: none -> 18.7 us  [send(): return lax.ppermute(value, AXES, pairs)]
    dot_general x5 -> x7, matrix products: 50.1 us -> 32.5 us  [the longest x4 19.6 us: body(): jnp.einsum('de,td->et', wkv, s, preferred_element_type=F32).astype(BF)]
    pallas_call x2 -> x3, Pallas kernels: 94.9 us -> 109 us  [the longest x1 57 us: attention_backward(): pl.pallas_call(functools.partial(backward_kernel, hd, tile, n), grid=(hea...]
    another operation x2 -> x1, other arithmetic: 12.8 us -> 1.93 us
  transfers between devices with their start and end apart: 28 -> 51, of which waited for: 6 -> 18; matrix products, arithmetic and copies ran while one was open for 30% -> 26% of each run, Pallas kernels for 15% -> 16%
where the time goes in v2:
time: 669 us; the launch traced here: 661 us
  waiting for transfers between devices  210 us (31%)
  starting transfers between devices  116 us (17%)
  Pallas kernels  109 us (16%)
  local copies, waits for them, and re-layouts  91 us (14%)
  matrix products  73.1 us (11%)
  other arithmetic  47.5 us (7%)
  between operations  15.2 us (2%)
    ppermute x47, waiting for transfers between devices, send(): return lax.ppermute(value, AXES, pairs)  209 us
    ppermute x47, starting transfers between devices, send(): return lax.ppermute(value, AXES, pairs)  115 us
    pallas_call x1, Pallas kernels, attention_backward(): pl.pallas_call(functools.partial(backward_kernel, hd, tile, n), grid=(hea...  57 us
    unnamed x93, local copies, waits for them, and re-layouts  36.3 us
    pallas_call x1, Pallas kernels, attention_forward(): pl.pallas_call(functools.partial(forward_kernel, hd, tile, n), grid=(head...  29.8 us
    pallas_call x1, Pallas kernels, input_gradient(): pl.pallas_call(functools.partial(dx_kernel, part, query_tiles), grid=(nk...  22.1 us
    dot_general x4, matrix products, body(): jnp.einsum('de,td->et', wkv, s, preferred_element_type=F32).astype(BF)  19.6 us
    ppermute x12, local copies, waits for them, and re-layouts, send(): return lax.ppermute(value, AXES, pairs)  18.7 us
  transfers between devices with their start and end apart: 51, of which 18 were waited for; matrix products, arithmetic and copies ran while one was open for 26% of the time, Pallas kernels for 16%

profile of v2, /device:TPU:0, one launch (start us, length us, event | category | flops | bytes accessed | tf_op | source)
XLA Modules:
  0.0 660.9 jit_solution(17530592995340581095)
XLA Ops:
  11.2 2.7 broadcast_in_dim.8
  15.1 2.9 collective-permute-start.3
  19.5 26.3 %collective-permute-done.3 = bf16[320,1920]{1,0:T(8,128)(2,1)S(1)} collective-permute-done((bf16[320,1920]{1,0:T(8,128)(2,1)S(1)}, bf16[320,1920]{1,0:T(8,128)(2,1)S(1)}, u32[]{:S(2)}, u32[]{:S(2)}) %collective-permute-start.3) | collective-permute-done | bytes 1228832 | tf_op jit(solution)/shard_map/ppermute | solution.py:404
  46.9 26.3 %collective-permute-done.4 = bf16[320,1920]{1,0:T(8,128)(2,1)} collective-permute-done((bf16[320,1920]{1,0:T(8,128)(2,1)S(1)}, bf16[320,1920]{1,0:T(8,128)(2,1)}, u32[]{:S(2)}, u32[]{:S(2)}) %collective-permute-start.4) | collective-permute-done | bytes 1228832 | tf_op jit(solution)/shard_map/ppermute | solution.py:404
  73.2 2.5 constant_dynamic-update-slice_fusion.4
  75.6 2.4 constant_dynamic-update-slice_fusion.3.w_ref
  80.5 30.1 %collective-permute-done = bf16[512,1280]{1,0:T(8,128)(2,1)S(1)} collective-permute-done((bf16[512,1280]{1,0:T(8,128)(2,1)S(1)}, bf16[512,1280]{1,0:T(8,128)(2,1)S(1)}, u32[]{:S(2)}, u32[]{:S(2)}) %collective-permute-start) | collective-permute-done | bytes 1310752 | tf_op jit(solution)/shard_map/ppermute | solution.py:404
  115.0 11.3 %collective-permute-start.11 = (bf16[512,1280]{1,0:T(8,128)(2,1)}, bf16[512,1280]{1,0:T(8,128)(2,1)}, u32[]{:S(2)}, u32[]{:S(2)}) collective-permute-start(bf16[512,1280]{1,0:T(8,128)(2,1)} %bitcast.6), channel_id=1, source_target_pairs={{0,0},{1,1},{2,5},{3,4},{4,3},{5,2},{6,6},{7,7},{8,8},{9,9},{10,13... | collective-permute-start | bytes 3932168 | tf_op jit(solution)/shard_map/ppermute | solution.py:404
  127.8 3.7 collective-permute-start.8
  136.7 3.0 fusion.13
  139.7 5.7 multiply_convert_fusion.2.refs_4_
  145.4 4.9 convolution_convert_fusion.9.refs_6_.refs_10_
  150.3 4.9 convolution_convert_fusion.10.refs_5_.refs_9_
  155.2 4.9 convolution_convert_fusion.7.refs_8_.refs_12_
  160.1 4.9 convolution_convert_fusion.8.refs_7_.refs_11_
  165.1 29.8 %attention_forward.1 = (f32[640,1024]{1,0:T(8,128)}, f32[8,1,1024]{2,1,0:T(1,128)}) custom-call(s32[2048]{0:T(1024)} %copy-done.25, s32[16]{0:T(128)} %fusion.26.refs_1_, s32[1,2048]{1,0:T(1,128)} %bitcast.60, s32[2048,1]{1,0:T(8,128)} %copy.37.refs_3_, bf16[640,1024]{1,0:T(8,128)(2,1)} %multiply_convert_fusion.2.refs_4_, ...), custom_call_target="tpu_custom_call" | custom-call | flops 10307921920 | bytes 16777216 | tf_op jit(solution)/shard_map/attention_forward/pallas_call | solution.py:194
  197.1 4.5 pad_maximum_fusion.1.x_ref
  202.5 4.6 multiply_reduce_fusion.2
  207.2 6.3 convolution_add_fusion.1
  213.5 5.5 convert_reduce_fusion.1
  221.0 2.2 multiply_reduce_fusion
  223.3 2.3 convert_reduce_fusion
  232.3 3.3 convolution_convert_fusion.2
  235.7 4.7 pad_maximum_fusion
  240.3 13.8 %copy.70 = bf16[1280,3840]{1,0:T(8,128)(2,1)} copy(bf16[1280,3840]{0,1:T(8,128)(2,1)} %pad_maximum_fusion) | data formatting | bytes 19660800
  255.4 57.0 %attention_backward.1 = (bf16[640,1024]{1,0:T(8,128)(2,1)}, bf16[640,2048]{1,0:T(8,128)(2,1)}, bf16[640,2048]{1,0:T(8,128)(2,1)}, f32[640,1]{1,0:T(8,128)}) custom-call(s32[2048]{0:T(1024)} %copy-done.25, s32[16]{0:T(128)} %fusion.26.refs_1_, s32[1,2048]{1,0:T(1,128)} %bitcast.61, s32[2048,1]{1,0:T(8,128)} %copy.37.refs_3_, ...), custom_call_target="tpu_custom_call" | custom-call | flops 25769803776 | bytes 33554432 | tf_op jit(solution)/shard_map/attention_backward/pallas_call | solution.py:225
  318.7 22.1 %input_gradient.1 = (bf16[2048,1280]{1,0:T(8,128)(2,1)}, f32[1,1280]{1,0:T(1,128)S(1)}) custom-call(bf16[640,1024]{1,0:T(8,128)(2,1)S(1)} %copy-done, bf16[640,2048]{1,0:T(8,128)(2,1)S(1)} %copy-done.4, bf16[640,2048]{1,0:T(8,128)(2,1)S(1)} %copy-done.2, bf16[1280,1920]{1,0:T(8,128)(2,1)} %constant_dynamic-update-slice_fusion.3.w_ref, ...), custom_call_target="tpu_custom_call" | custom-call | flops 8388608000 | bytes 25165824 | tf_op jit(solution)/shard_map/input_gradient/pallas_call | solution.py:290
  341.3 6.3 convolution_convert_fusion.4
  347.7 4.7 convolution_convert_fusion.3
  355.2 2.9 collective-permute-done.42
  358.2 2.4 collective-permute-start.43
  360.6 3.8 constant_dynamic-slice_fusion.5
  364.4 2.5 copy.41
  374.5 6.7 %collective-permute-start.44 = (f32[48,128]{1,0:T(8,128)S(1)}, f32[48,128]{1,0:T(8,128)S(1)}, u32[]{:S(2)}, u32[]{:S(2)}) collective-permute-start(f32[48,128]{1,0:T(8,128)S(1)} %add.292), channel_id=1, source_target_pairs={{0,1},{3,2},{4,5},{7,6},{8,9},{11,10},{12,13},{15,14},{16,17},{19,... | collective-permute-start | bytes 73736 | tf_op jit(solution)/shard_map/ppermute | solution.py:404
  381.1 6.8 %fusion.4 = bf16[512,1280]{1,0:T(8,128)(2,1)} fusion(f32[512,1280]{1,0:T(8,128)} %copy-done.11, bf16[1280,1280]{1,0:T(8,128)(2,1)} %all-gather.8.cloned.1.call-done, f32[1280]{0:T(1024)S(1)} %copy-done.28, f32[512,1280]{1,0:T(8,128)} %convolution_add_fusion.1), kind=kOutput, calls=%fused_computation.29 | convolution fusion | flops 1682964480 | bytes 9835520 | tf_op jit(solution)/shard_map/dot_general | solution.py:518
  387.9 11.3 %collective-permute-start.10 = (bf16[512,1280]{1,0:T(8,128)(2,1)}, bf16[512,1280]{1,0:T(8,128)(2,1)}, u32[]{:S(2)}, u32[]{:S(2)}) collective-permute-start(bf16[512,1280]{1,0:T(8,128)(2,1)} %fusion.4), channel_id=1, source_target_pairs={{0,0},{1,1},{2,5},{3,4},{4,3},{5,2},{6,6},{7,7},{8,8},{9,9},{10,13... | collective-permute-start | bytes 3932168 | tf_op jit(solution)/shard_map/ppermute | solution.py:404
  401.6 8.0 %collective-permute-start.14 = (bf16[512,1280]{1,0:T(8,128)(2,1)}, bf16[512,1280]{1,0:T(8,128)(2,1)}, u32[]{:S(2)}, u32[]{:S(2)}) collective-permute-start(bf16[512,1280]{1,0:T(8,128)(2,1)} %get-tuple-element.75), channel_id=1, source_target_pairs={{0,4},{1,5},{2,6},{3,7},{4,0},{5,1},{6,2},{7,3},{8,12},{9,13},{10,... | collective-permute-start | bytes 3932168 | tf_op jit(solution)/shard_map/ppermute | solution.py:404
  409.7 15.1 %collective-permute-done.18 = bf16[320,1920]{1,0:T(8,128)(2,1)S(1)} collective-permute-done((bf16[320,1920]{1,0:T(8,128)(2,1)}, bf16[320,1920]{1,0:T(8,128)(2,1)S(1)}, u32[]{:S(2)}, u32[]{:S(2)}) %collective-permute-start.18) | collective-permute-done | bytes 1228832 | tf_op jit(solution)/shard_map/ppermute | solution.py:404
  427.1 2.7 copy.44
  429.8 2.3 copy.46
  432.2 2.5 copy.42
  434.7 3.2 convert_add_fusion.2
  438.1 13.3 %collective-permute-start.28 = (bf16[320,640]{0,1:T(8,128)(2,1)S(1)}, bf16[320,640]{0,1:T(8,128)(2,1)S(1)}, u32[]{:S(2)}, u32[]{:S(2)}) collective-permute-start(bf16[320,640]{0,1:T(8,128)(2,1)S(1)} %get-tuple-element.82), channel_id=1, source_target_pairs={{0,1},{3,2},{4,5},{7,6},{8,9},{11,10},{12,13},{15,14},{16,17},{19,... | collective-permute-start | bytes 1228808 | tf_op jit(solution)/shard_map/ppermute | solution.py:404
  455.5 7.4 %collective-permute-done.28 = bf16[320,640]{0,1:T(8,128)(2,1)S(1)} collective-permute-done((bf16[320,640]{0,1:T(8,128)(2,1)S(1)}, bf16[320,640]{0,1:T(8,128)(2,1)S(1)}, u32[]{:S(2)}, u32[]{:S(2)}) %collective-permute-start.28) | collective-permute-done | bytes 409632 | tf_op jit(solution)/shard_map/ppermute | solution.py:404
  462.9 10.5 %collective-permute-done.24 = bf16[320,640]{0,1:T(8,128)(2,1)S(1)} collective-permute-done((bf16[320,640]{0,1:T(8,128)(2,1)S(1)}, bf16[320,640]{0,1:T(8,128)(2,1)S(1)}, u32[]{:S(2)}, u32[]{:S(2)}) %collective-permute-start.24) | collective-permute-done | bytes 409632 | tf_op jit(solution)/shard_map/ppermute | solution.py:404
  473.5 10.1 %collective-permute-done.20 = bf16[320,640]{0,1:T(8,128)(2,1)S(1)} collective-permute-done((bf16[320,640]{0,1:T(8,128)(2,1)S(1)}, bf16[320,640]{0,1:T(8,128)(2,1)S(1)}, u32[]{:S(2)}, u32[]{:S(2)}) %collective-permute-start.20) | collective-permute-done | bytes 409632 | tf_op jit(solution)/shard_map/ppermute | solution.py:404
  492.9 30.1 %collective-permute-done.30 = bf16[320,640]{0,1:T(8,128)(2,1)S(1)} collective-permute-done((bf16[320,640]{0,1:T(8,128)(2,1)S(1)}, bf16[320,640]{0,1:T(8,128)(2,1)S(1)}, u32[]{:S(2)}, u32[]{:S(2)}) %collective-permute-start.30) | collective-permute-done | bytes 409632 | tf_op jit(solution)/shard_map/ppermute | solution.py:404
  523.3 6.3 collective-permute-start.31
  529.6 3.9 collective-permute-done.22
  533.8 6.3 collective-permute-start.23
  540.2 3.9 collective-permute-done.26
  544.3 3.0 collective-permute-start.27
  547.3 3.9 select_convert_fusion
  556.8 3.9 copy.65
  560.7 2.3 fusion.37
  563.1 4.7 collective-permute-start.38
  567.7 11.5 %collective-permute-done.16 = bf16[512,1280]{1,0:T(8,128)(2,1)} collective-permute-done((bf16[512,1280]{1,0:T(8,128)(2,1)}, bf16[512,1280]{1,0:T(8,128)(2,1)}, u32[]{:S(2)}, u32[]{:S(2)}) %collective-permute-start.16) | collective-permute-done | bytes 1310752 | tf_op jit(solution)/shard_map/ppermute | solution.py:404
  579.2 3.8 fusion.17
  598.5 5.0 collective-permute-done.32
  618.5 14.9 %collective-permute-done.40 = bf16[160,1280]{1,0:T(8,128)(2,1)} collective-permute-done((bf16[160,1280]{1,0:T(8,128)(2,1)}, bf16[160,1280]{1,0:T(8,128)(2,1)}, u32[]{:S(2)}, u32[]{:S(2)}) %collective-permute-start.40) | collective-permute-done | bytes 409632 | tf_op jit(solution)/shard_map/ppermute | solution.py:404
  635.7 2.6 copy.68
  638.3 3.8 collective-permute-done.37
  644.7 4.4 collective-permute-done.34
  651.7 2.5 copy.90
  (267 shorter events, 113.6 us)
Async XLA Ops:
  7.2 195.3 %all-gather.4.cloned.1.call-start = ((), (), s32[]{:S(2)}) async-start(), calls=%async_computation.1 | async-start | bytes 3686400 | tf_op jit(solution)/shard_map/all_gather | solution.py:480
  8.8 2.2 collective-permute-start.2
  15.1 30.7 %collective-permute-start.3 = (bf16[320,1920]{1,0:T(8,128)(2,1)S(1)}, bf16[320,1920]{1,0:T(8,128)(2,1)S(1)}, u32[]{:S(2)}, u32[]{:S(2)}) collective-permute-start(bf16[320,1920]{1,0:T(8,128)(2,1)S(1)} %get-tuple-element.94), channel_id=1, source_target_pairs={{0,8},{1,9},{2,10},{3,11},{4,12},{5,13},{6,14},{7,15},{8,0},{9,1},... | collective-permute-start | bytes 3686408 | tf_op jit(solution)/shard_map/ppermute | solution.py:404
  17.9 55.2 %collective-permute-start.4 = (bf16[320,1920]{1,0:T(8,128)(2,1)S(1)}, bf16[320,1920]{1,0:T(8,128)(2,1)}, u32[]{:S(2)}, u32[]{:S(2)}) collective-permute-start(bf16[320,1920]{1,0:T(8,128)(2,1)S(1)} %get-tuple-element.94), channel_id=1, source_target_pairs={{0,16},{1,17},{2,18},{3,19},{4,20},{5,21},{6,22},{7,23},{8,24},{9,... | collective-permute-start | bytes 3686408 | tf_op jit(solution)/shard_map/ppermute | solution.py:404
  19.5 56.2 %collective-permute-start.5 = (bf16[320,1920]{1,0:T(8,128)(2,1)S(1)}, bf16[320,1920]{1,0:T(8,128)(2,1)}, u32[]{:S(2)}, u32[]{:S(2)}) collective-permute-start(bf16[320,1920]{1,0:T(8,128)(2,1)S(1)} %get-tuple-element.94), channel_id=1, source_target_pairs={{0,24},{1,25},{2,26},{3,27},{4,28},{5,29},{6,30},{7,31},{8,16},{9,... | collective-permute-start | bytes 3686408 | tf_op jit(solution)/shard_map/ppermute | solution.py:404
  46.9 32.0 %copy-start.21 = (bf16[1,512,1280]{2,1,0:T(8,128)(2,1)S(1)}, bf16[1,512,1280]{2,1,0:T(8,128)(2,1)}, u32[]{:S(2)}) copy-start(bf16[1,512,1280]{2,1,0:T(8,128)(2,1)} %param.13) | copy-start | bytes 3932164
  78.0 36.9 %copy-start.27 = (s32[1,2048]{1,0:T(1,128)S(1)}, s32[1,2048]{1,0:T(1,128)}, u32[]{:S(2)}) copy-start(s32[1,2048]{1,0:T(1,128)} %param.14) | copy-start | bytes 24580
  78.1 129.1 %all-gather.6.cloned.1.call-start = ((), (), s32[]{:S(2)}) async-start(), calls=%async_computation.2 | async-start | bytes 3686400 | tf_op jit(solution)/shard_map/all_gather | solution.py:481
  78.8 134.7 %all-gather.8.cloned.1.call-start = ((), (), s32[]{:S(2)}) async-start(), calls=%async_computation.3 | async-start | bytes 3686400 | tf_op jit(solution)/shard_map/all_gather | solution.py:482
  78.9 31.7 %collective-permute-start = (bf16[512,1280]{1,0:T(8,128)(2,1)S(1)}, bf16[512,1280]{1,0:T(8,128)(2,1)S(1)}, u32[]{:S(2)}, u32[]{:S(2)}) collective-permute-start(bf16[512,1280]{1,0:T(8,128)(2,1)S(1)} %bitcast.57), channel_id=1, source_target_pairs={{0,1},{1,0},{2,5},{3,4},{4,3},{5,2},{6,7},{7,6},{8,9},{9,8},{10,13... | collective-permute-start | bytes 3932168 | tf_op jit(solution)/shard_map/ppermute | solution.py:404
  112.1 20.7 %copy-start.26 = (bf16[1280]{0:T(1024)(128)(2,1)S(1)}, bf16[1280]{0:T(1024)(128)(2,1)}, u32[]{:S(2)}) copy-start(bf16[1280]{0:T(1024)(128)(2,1)} %param.19) | copy-start | bytes 7684
  112.1 20.8 %copy-start.29 = (bf16[1280]{0:T(1024)(128)(2,1)S(1)}, bf16[1280]{0:T(1024)(128)(2,1)}, u32[]{:S(2)}) copy-start(bf16[1280]{0:T(1024)(128)(2,1)} %param.20) | copy-start | bytes 7684
  112.1 20.8 %copy-start.30 = (bf16[1280]{0:T(1024)(128)(2,1)S(1)}, bf16[1280]{0:T(1024)(128)(2,1)}, u32[]{:S(2)}) copy-start(bf16[1280]{0:T(1024)(128)(2,1)} %param.21) | copy-start | bytes 7684
  112.1 20.8 %copy-start.31 = (bf16[1280]{0:T(1024)(128)(2,1)S(1)}, bf16[1280]{0:T(1024)(128)(2,1)}, u32[]{:S(2)}) copy-start(bf16[1280]{0:T(1024)(128)(2,1)} %param.22) | copy-start | bytes 7684
  112.1 14.2 %collective-permute-start.7 = (bf16[512,1280]{1,0:T(8,128)(2,1)}, bf16[512,1280]{1,0:T(8,128)(2,1)S(1)}, u32[]{:S(2)}, u32[]{:S(2)}) collective-permute-start(bf16[512,1280]{1,0:T(8,128)(2,1)} %get-tuple-element.73), channel_id=1, source_target_pairs={{2,3},{3,2},{4,5},{5,4},{10,11},{11,10},{12,13},{13,12},{18,19},{1... | collective-permute-start | bytes 3932168 | tf_op jit(solution)/shard_map/ppermute | solution.py:404
  113.0 22.9 %collective-permute-start.6 = (bf16[512,1280]{1,0:T(8,128)(2,1)}, bf16[512,1280]{1,0:T(8,128)(2,1)S(1)}, u32[]{:S(2)}, u32[]{:S(2)}) collective-permute-start(bf16[512,1280]{1,0:T(8,128)(2,1)} %get-tuple-element.73), channel_id=1, source_target_pairs={{0,4},{1,5},{2,6},{3,7},{4,0},{5,1},{6,2},{7,3},{8,12},{9,13},{10,... | collective-permute-start | bytes 3932168 | tf_op jit(solution)/shard_map/ppermute | solution.py:404
  114.9 19.5 %collective-permute-start.1 = (s32[2048]{0:T(1024)S(1)}, s32[2048]{0:T(1024)S(1)}, u32[]{:S(2)}, u32[]{:S(2)}) collective-permute-start(s32[2048]{0:T(1024)S(1)} %bitcast.62), channel_id=1, source_target_pairs={{0,4},{1,5},{2,6},{3,7},{4,0},{5,1},{6,2},{7,3},{8,12},{9,13},{10,... | collective-permute-start | bytes 24584 | tf_op jit(solution)/shard_map/ppermute | solution.py:404
  115.0 98.5 %collective-permute-start.11 = (bf16[512,1280]{1,0:T(8,128)(2,1)}, bf16[512,1280]{1,0:T(8,128)(2,1)}, u32[]{:S(2)}, u32[]{:S(2)}) collective-permute-start(bf16[512,1280]{1,0:T(8,128)(2,1)} %bitcast.6), channel_id=1, source_target_pairs={{0,0},{1,1},{2,5},{3,4},{4,3},{5,2},{6,6},{7,7},{8,8},{9,9},{10,13... | collective-permute-start | bytes 3932168 | tf_op jit(solution)/shard_map/ppermute | solution.py:404
  127.8 8.5 %collective-permute-start.8 = (bf16[512,1280]{1,0:T(8,128)(2,1)}, bf16[512,1280]{1,0:T(8,128)(2,1)S(1)}, u32[]{:S(2)}, u32[]{:S(2)}) collective-permute-start(bf16[512,1280]{1,0:T(8,128)(2,1)} %get-tuple-element.71), channel_id=1, source_target_pairs={{0,4},{1,5},{2,6},{3,7},{4,0},{5,1},{6,2},{7,3},{8,12},{9,13},{10,... | collective-permute-start | bytes 3932168 | tf_op jit(solution)/shard_map/ppermute | solution.py:404
  135.9 424.8 %reduce-scatter.4.cloned.1.call-start = ((), (), s32[]{:S(2)}) async-start(), calls=%async_computation.4 | async-start | bytes 11059200
  139.7 20.4 %copy-start.19 = (bf16[512,1280]{1,0:T(8,128)(2,1)}, bf16[512,1280]{1,0:T(8,128)(2,1)S(1)}, u32[]{:S(2)}) copy-start(bf16[512,1280]{1,0:T(8,128)(2,1)S(1)} %get-tuple-element.109) | copy-start | bytes 3932164
  196.9 4.6 collective-permute-start.9
  230.7 23.5 %collective-permute-start.12 = (bf16[640,512]{1,0:T(8,128)(2,1)S(1)}, bf16[640,512]{1,0:T(8,128)(2,1)S(1)}, u32[]{:S(2)}, u32[]{:S(2)}) collective-permute-start(bf16[640,512]{1,0:T(8,128)(2,1)S(1)} %get-tuple-element.90), channel_id=1, source_target_pairs={{0,4},{1,5},{2,6},{3,7},{4,0},{5,1},{6,2},{7,3},{8,12},{9,13},{10,... | collective-permute-start | bytes 1966088 | tf_op jit(solution)/shard_map/ppermute | solution.py:404
  318.7 22.6 %copy-start.5 = (bf16[640,2048]{1,0:T(8,128)(2,1)S(1)}, bf16[640,2048]{1,0:T(8,128)(2,1)}, u32[]{:S(2)}) copy-start(bf16[640,2048]{1,0:T(8,128)(2,1)} %get-tuple-element.30.dk_ref) | copy-start | bytes 7864324
  341.0 13.3 %collective-permute-start.41 = (f32[48,128]{1,0:T(8,128)S(1)}, f32[48,128]{1,0:T(8,128)S(1)}, u32[]{:S(2)}, u32[]{:S(2)}) collective-permute-start(f32[48,128]{1,0:T(8,128)S(1)} %pad_bitcast_fusion), channel_id=1, source_target_pairs={{0,4},{1,5},{2,6},{3,7},{4,0},{5,1},{6,2},{7,3},{8,12},{9,13},{10,... | collective-permute-start | bytes 73736 | tf_op jit(solution)/shard_map/ppermute | solution.py:404
  354.3 3.9 collective-permute-start.42
  358.2 16.3 %collective-permute-start.43 = (f32[48,128]{1,0:T(8,128)S(1)}, f32[48,128]{1,0:T(8,128)S(1)}, u32[]{:S(2)}, u32[]{:S(2)}) collective-permute-start(f32[48,128]{1,0:T(8,128)S(1)} %fusion.55), channel_id=1, source_target_pairs={{0,16},{1,17},{2,18},{3,19},{4,20},{5,21},{6,22},{7,23},{8,24},{9,... | collective-permute-start | bytes 73736 | tf_op jit(solution)/shard_map/ppermute | solution.py:404
  370.9 53.8 %collective-permute-start.18 = (bf16[320,1920]{1,0:T(8,128)(2,1)}, bf16[320,1920]{1,0:T(8,128)(2,1)S(1)}, u32[]{:S(2)}, u32[]{:S(2)}) collective-permute-start(bf16[320,1920]{1,0:T(8,128)(2,1)} %copy.43), channel_id=1, source_target_pairs={{0,16},{1,17},{2,18},{3,19},{4,20},{5,21},{6,22},{7,23},{8,24},{9,... | collective-permute-start | bytes 3686408 | tf_op jit(solution)/shard_map/ppermute | solution.py:404
  371.0 58.8 %collective-permute-start.19 = (bf16[320,1920]{1,0:T(8,128)(2,1)S(1)}, bf16[320,1920]{1,0:T(8,128)(2,1)}, u32[]{:S(2)}, u32[]{:S(2)}) collective-permute-start(bf16[320,1920]{1,0:T(8,128)(2,1)S(1)} %copy-done.22), channel_id=1, source_target_pairs={{0,24},{1,25},{2,26},{3,27},{4,28},{5,29},{6,30},{7,31},{8,16},{9,... | collective-permute-start | bytes 3686408 | tf_op jit(solution)/shard_map/ppermute | solution.py:404
  372.4 59.8 %collective-permute-start.17 = (bf16[320,1920]{1,0:T(8,128)(2,1)}, bf16[320,1920]{1,0:T(8,128)(2,1)}, u32[]{:S(2)}, u32[]{:S(2)}) collective-permute-start(bf16[320,1920]{1,0:T(8,128)(2,1)} %copy.41), channel_id=1, source_target_pairs={{0,8},{1,9},{2,10},{3,11},{4,12},{5,13},{6,14},{7,15},{8,0},{9,1},... | collective-permute-start | bytes 3686408 | tf_op jit(solution)/shard_map/ppermute | solution.py:404
  374.4 25.5 %slice-start = ((s8[5242880]{0:T(1024)(128)(4,1)}), s8[4194304]{0:T(1024)(128)(4,1)S(1)}, s32[]{:S(2)}) async-start(s8[5242880]{0:T(1024)(128)(4,1)} %bitcast.53), calls=%async_computation.5 | async-start | bytes 8388608
  374.5 25.5 %slice-start.1 = ((s8[5242880]{0:T(1024)(128)(4,1)}), s8[1048576]{0:T(1024)(128)(4,1)S(1)}, s32[]{:S(2)}) async-start(s8[5242880]{0:T(1024)(128)(4,1)} %bitcast.53), calls=%async_computation.6 | async-start | bytes 2097152
  374.5 24.8 %collective-permute-start.44 = (f32[48,128]{1,0:T(8,128)S(1)}, f32[48,128]{1,0:T(8,128)S(1)}, u32[]{:S(2)}, u32[]{:S(2)}) collective-permute-start(f32[48,128]{1,0:T(8,128)S(1)} %add.292), channel_id=1, source_target_pairs={{0,1},{3,2},{4,5},{7,6},{8,9},{11,10},{12,13},{15,14},{16,17},{19,... | collective-permute-start | bytes 73736 | tf_op jit(solution)/shard_map/ppermute | solution.py:404
  387.9 67.3 %collective-permute-start.10 = (bf16[512,1280]{1,0:T(8,128)(2,1)}, bf16[512,1280]{1,0:T(8,128)(2,1)}, u32[]{:S(2)}, u32[]{:S(2)}) collective-permute-start(bf16[512,1280]{1,0:T(8,128)(2,1)} %fusion.4), channel_id=1, source_target_pairs={{0,0},{1,1},{2,5},{3,4},{4,3},{5,2},{6,6},{7,7},{8,8},{9,9},{10,13... | collective-permute-start | bytes 3932168 | tf_op jit(solution)/shard_map/ppermute | solution.py:404
  399.2 2.4 collective-permute-start.45
  401.6 83.8 %collective-permute-start.14 = (bf16[512,1280]{1,0:T(8,128)(2,1)}, bf16[512,1280]{1,0:T(8,128)(2,1)}, u32[]{:S(2)}, u32[]{:S(2)}) collective-permute-start(bf16[512,1280]{1,0:T(8,128)(2,1)} %get-tuple-element.75), channel_id=1, source_target_pairs={{0,4},{1,5},{2,6},{3,7},{4,0},{5,1},{6,2},{7,3},{8,12},{9,13},{10,... | collective-permute-start | bytes 3932168 | tf_op jit(solution)/shard_map/ppermute | solution.py:404
  425.8 27.0 %collective-permute-start.46 = (f32[48,128]{1,0:T(8,128)S(1)}, f32[48,128]{1,0:T(8,128)S(1)}, u32[]{:S(2)}, u32[]{:S(2)}) collective-permute-start(f32[48,128]{1,0:T(8,128)S(1)} %add.294), channel_id=1, source_target_pairs={{1,0},{2,3},{5,4},{6,7},{9,8},{10,11},{13,12},{14,15},{17,16},{18,... | collective-permute-start | bytes 73736 | tf_op jit(solution)/shard_map/ppermute | solution.py:404
  434.7 50.7 %slice-start.2 = ((s8[5242880]{0:T(1024)(128)(4,1)}), s8[4194304]{0:T(1024)(128)(4,1)S(1)}, s32[]{:S(2)}) async-start(s8[5242880]{0:T(1024)(128)(4,1)} %bitcast.55), calls=%async_computation.7 | async-start | bytes 8388608
  437.9 47.5 %slice-start.3 = ((s8[5242880]{0:T(1024)(128)(4,1)}), s8[1048576]{0:T(1024)(128)(4,1)S(1)}, s32[]{:S(2)}) async-start(s8[5242880]{0:T(1024)(128)(4,1)} %bitcast.55), calls=%async_computation.8 | async-start | bytes 2097152
  438.1 24.8 %collective-permute-start.28 = (bf16[320,640]{0,1:T(8,128)(2,1)S(1)}, bf16[320,640]{0,1:T(8,128)(2,1)S(1)}, u32[]{:S(2)}, u32[]{:S(2)}) collective-permute-start(bf16[320,640]{0,1:T(8,128)(2,1)S(1)} %get-tuple-element.82), channel_id=1, source_target_pairs={{0,1},{3,2},{4,5},{7,6},{8,9},{11,10},{12,13},{15,14},{16,17},{19,... | collective-permute-start | bytes 1228808 | tf_op jit(solution)/shard_map/ppermute | solution.py:404
  451.4 22.0 %collective-permute-start.24 = (bf16[320,640]{0,1:T(8,128)(2,1)S(1)}, bf16[320,640]{0,1:T(8,128)(2,1)S(1)}, u32[]{:S(2)}, u32[]{:S(2)}) collective-permute-start(bf16[320,640]{0,1:T(8,128)(2,1)S(1)} %get-tuple-element.83), channel_id=1, source_target_pairs={{0,1},{3,2},{4,5},{7,6},{8,9},{11,10},{12,13},{15,14},{16,17},{19,... | collective-permute-start | bytes 1228808 | tf_op jit(solution)/shard_map/ppermute | solution.py:404
  452.8 30.8 %collective-permute-start.20 = (bf16[320,640]{0,1:T(8,128)(2,1)S(1)}, bf16[320,640]{0,1:T(8,128)(2,1)S(1)}, u32[]{:S(2)}, u32[]{:S(2)}) collective-permute-start(bf16[320,640]{0,1:T(8,128)(2,1)S(1)} %get-tuple-element.84), channel_id=1, source_target_pairs={{0,1},{3,2},{4,5},{7,6},{8,9},{11,10},{12,13},{15,14},{16,17},{19,... | collective-permute-start | bytes 1228808 | tf_op jit(solution)/shard_map/ppermute | solution.py:404
  455.2 92.1 %collective-permute-start.13 = (bf16[512,1280]{1,0:T(8,128)(2,1)S(1)}, bf16[512,1280]{1,0:T(8,128)(2,1)S(1)}, u32[]{:S(2)}, u32[]{:S(2)}) collective-permute-start(bf16[512,1280]{1,0:T(8,128)(2,1)S(1)} %copy-done.12), channel_id=1, source_target_pairs={{0,4},{1,5},{2,6},{3,7},{4,0},{5,1},{6,2},{7,3},{8,12},{9,13},{10,... | collective-permute-start | bytes 3932168 | tf_op jit(solution)/shard_map/ppermute | solution.py:404
  484.0 4.6 collective-permute-start.29
  484.7 5.3 collective-permute-start.21
  487.1 60.2 %collective-permute-start.15 = (bf16[512,1280]{1,0:T(8,128)(2,1)S(1)}, bf16[512,1280]{1,0:T(8,128)(2,1)S(1)}, u32[]{:S(2)}, u32[]{:S(2)}) collective-permute-start(bf16[512,1280]{1,0:T(8,128)(2,1)S(1)} %fusion.18), channel_id=1, source_target_pairs={{2,3},{3,2},{4,5},{5,4},{10,11},{11,10},{12,13},{13,12},{18,19},{1... | collective-permute-start | bytes 3932168 | tf_op jit(solution)/shard_map/ppermute | solution.py:404
  487.9 3.6 collective-permute-start.25
  488.7 34.3 %collective-permute-start.30 = (bf16[320,640]{0,1:T(8,128)(2,1)S(1)}, bf16[320,640]{0,1:T(8,128)(2,1)S(1)}, u32[]{:S(2)}, u32[]{:S(2)}) collective-permute-start(bf16[320,640]{0,1:T(8,128)(2,1)S(1)} %add_convert_fusion.6), channel_id=1, source_target_pairs={{1,0},{2,3},{5,4},{6,7},{9,8},{10,11},{13,12},{14,15},{17,16},{18,... | collective-permute-start | bytes 1228808 | tf_op jit(solution)/shard_map/ppermute | solution.py:404
  490.2 43.4 %collective-permute-start.22 = (bf16[320,640]{0,1:T(8,128)(2,1)S(1)}, bf16[320,640]{0,1:T(8,128)(2,1)S(1)}, u32[]{:S(2)}, u32[]{:S(2)}) collective-permute-start(bf16[320,640]{0,1:T(8,128)(2,1)S(1)} %add_convert_fusion.10), channel_id=1, source_target_pairs={{1,0},{2,3},{5,4},{6,7},{9,8},{10,11},{13,12},{14,15},{17,16},{18,... | collective-permute-start | bytes 1228808 | tf_op jit(solution)/shard_map/ppermute | solution.py:404
  491.6 52.5 %collective-permute-start.26 = (bf16[320,640]{0,1:T(8,128)(2,1)S(1)}, bf16[320,640]{0,1:T(8,128)(2,1)S(1)}, u32[]{:S(2)}, u32[]{:S(2)}) collective-permute-start(bf16[320,640]{0,1:T(8,128)(2,1)S(1)} %add_convert_fusion.8), channel_id=1, source_target_pairs={{1,0},{2,3},{5,4},{6,7},{9,8},{10,11},{13,12},{14,15},{17,16},{18,... | collective-permute-start | bytes 1228808 | tf_op jit(solution)/shard_map/ppermute | solution.py:404
  523.1 24.2 %copy-start.8 = (f32[512,1280]{1,0:T(8,128)S(1)}, f32[512,1280]{1,0:T(8,128)}, u32[]{:S(2)}) copy-start(f32[512,1280]{1,0:T(8,128)} %copy-done.7) | copy-start | bytes 7864324
  523.3 31.7 %collective-permute-start.31 = (bf16[160,640]{0,1:T(8,128)(2,1)S(1)}, bf16[160,640]{0,1:T(8,128)(2,1)S(1)}, u32[]{:S(2)}, u32[]{:S(2)}) collective-permute-start(bf16[160,640]{0,1:T(8,128)(2,1)S(1)} %constant_dynamic-slice_fusion), channel_id=1, source_target_pairs={{0,4},{1,5},{2,6},{3,7},{4,0},{5,1},{6,2},{7,3},{8,12},{9,13},{10,... | collective-permute-start | bytes 614408 | tf_op jit(solution)/shard_map/ppermute | solution.py:404
  533.8 17.5 %collective-permute-start.23 = (bf16[160,640]{0,1:T(8,128)(2,1)S(1)}, bf16[160,640]{0,1:T(8,128)(2,1)S(1)}, u32[]{:S(2)}, u32[]{:S(2)}) collective-permute-start(bf16[160,640]{0,1:T(8,128)(2,1)S(1)} %constant_dynamic-slice_fusion.2), channel_id=1, source_target_pairs={{0,4},{1,5},{2,6},{3,7},{4,0},{5,1},{6,2},{7,3},{8,12},{9,13},{10,... | collective-permute-start | bytes 614408 | tf_op jit(solution)/shard_map/ppermute | solution.py:404
  544.3 8.8 %collective-permute-start.27 = (bf16[160,640]{0,1:T(8,128)(2,1)S(1)}, bf16[160,640]{0,1:T(8,128)(2,1)S(1)}, u32[]{:S(2)}, u32[]{:S(2)}) collective-permute-start(bf16[160,640]{0,1:T(8,128)(2,1)S(1)} %constant_dynamic-slice_fusion.1), channel_id=1, source_target_pairs={{0,4},{1,5},{2,6},{3,7},{4,0},{5,1},{6,2},{7,3},{8,12},{9,13},{10,... | collective-permute-start | bytes 614408 | tf_op jit(solution)/shard_map/ppermute | solution.py:404
  551.3 27.9 %collective-permute-start.16 = (bf16[512,1280]{1,0:T(8,128)(2,1)}, bf16[512,1280]{1,0:T(8,128)(2,1)}, u32[]{:S(2)}, u32[]{:S(2)}) collective-permute-start(bf16[512,1280]{1,0:T(8,128)(2,1)} %select_convert_fusion), channel_id=1, source_target_pairs={{0,1},{1,0},{2,5},{3,4},{4,3},{5,2},{6,7},{7,6},{8,9},{9,8},{10,13... | collective-permute-start | bytes 3932168 | tf_op jit(solution)/shard_map/ppermute | solution.py:404
  563.1 26.8 %collective-permute-start.38 = (bf16[160,1280]{1,0:T(8,128)(2,1)S(1)}, bf16[160,1280]{1,0:T(8,128)(2,1)}, u32[]{:S(2)}, u32[]{:S(2)}) collective-permute-start(bf16[160,1280]{1,0:T(8,128)(2,1)S(1)} %get-tuple-element.91), channel_id=1, source_target_pairs={{0,1},{3,2},{4,5},{7,6},{8,9},{11,10},{12,13},{15,14},{16,17},{19,... | collective-permute-start | bytes 1228808 | tf_op jit(solution)/shard_map/ppermute | solution.py:404
  583.3 11.4 %collective-permute-start.35 = (bf16[160,1280]{1,0:T(8,128)(2,1)}, bf16[160,1280]{1,0:T(8,128)(2,1)}, u32[]{:S(2)}, u32[]{:S(2)}) collective-permute-start(bf16[160,1280]{1,0:T(8,128)(2,1)} %get-tuple-element.92), channel_id=1, source_target_pairs={{0,1},{3,2},{4,5},{7,6},{8,9},{11,10},{12,13},{15,14},{16,17},{19,... | collective-permute-start | bytes 1228808 | tf_op jit(solution)/shard_map/ppermute | solution.py:404
  586.6 16.9 %collective-permute-start.32 = (bf16[160,1280]{1,0:T(8,128)(2,1)}, bf16[160,1280]{1,0:T(8,128)(2,1)}, u32[]{:S(2)}, u32[]{:S(2)}) collective-permute-start(bf16[160,1280]{1,0:T(8,128)(2,1)} %get-tuple-element.93), channel_id=1, source_target_pairs={{0,1},{3,2},{4,5},{7,6},{8,9},{11,10},{12,13},{15,14},{16,17},{19,... | collective-permute-start | bytes 1228808 | tf_op jit(solution)/shard_map/ppermute | solution.py:404
  592.3 15.2 %collective-permute-start.39 = (bf16[160,1280]{1,0:T(8,128)(2,1)}, bf16[160,1280]{1,0:T(8,128)(2,1)}, u32[]{:S(2)}, u32[]{:S(2)}) collective-permute-start(bf16[160,1280]{1,0:T(8,128)(2,1)} %copy.61), channel_id=1, source_target_pairs={{1,2},{2,1},{5,6},{6,5},{9,10},{10,9},{13,14},{14,13},{17,18},{18,... | collective-permute-start | bytes 1228808 | tf_op jit(solution)/shard_map/ppermute | solution.py:404
  597.1 14.0 %collective-permute-start.36 = (bf16[160,1280]{1,0:T(8,128)(2,1)}, bf16[160,1280]{1,0:T(8,128)(2,1)}, u32[]{:S(2)}, u32[]{:S(2)}) collective-permute-start(bf16[160,1280]{1,0:T(8,128)(2,1)} %copy.55), channel_id=1, source_target_pairs={{1,2},{2,1},{5,6},{6,5},{9,10},{10,9},{13,14},{14,13},{17,18},{18,... | collective-permute-start | bytes 1228808 | tf_op jit(solution)/shard_map/ppermute | solution.py:404
  605.8 8.9 %collective-permute-start.33 = (bf16[160,1280]{1,0:T(8,128)(2,1)}, bf16[160,1280]{1,0:T(8,128)(2,1)}, u32[]{:S(2)}, u32[]{:S(2)}) collective-permute-start(bf16[160,1280]{1,0:T(8,128)(2,1)} %copy.49), channel_id=1, source_target_pairs={{1,2},{2,1},{5,6},{6,5},{9,10},{10,9},{13,14},{14,13},{17,18},{18,... | collective-permute-start | bytes 1228808 | tf_op jit(solution)/shard_map/ppermute | solution.py:404
  609.8 23.5 %collective-permute-start.40 = (bf16[160,1280]{1,0:T(8,128)(2,1)}, bf16[160,1280]{1,0:T(8,128)(2,1)}, u32[]{:S(2)}, u32[]{:S(2)}) collective-permute-start(bf16[160,1280]{1,0:T(8,128)(2,1)} %copy.63), channel_id=1, source_target_pairs={{1,0},{2,3},{5,4},{6,7},{9,8},{10,11},{13,12},{14,15},{17,16},{18,... | collective-permute-start | bytes 1228808 | tf_op jit(solution)/shard_map/ppermute | solution.py:404
  613.5 28.6 %collective-permute-start.37 = (bf16[160,1280]{1,0:T(8,128)(2,1)}, bf16[160,1280]{1,0:T(8,128)(2,1)}, u32[]{:S(2)}, u32[]{:S(2)}) collective-permute-start(bf16[160,1280]{1,0:T(8,128)(2,1)} %copy.57), channel_id=1, source_target_pairs={{1,0},{2,3},{5,4},{6,7},{9,8},{10,11},{13,12},{14,15},{17,16},{18,... | collective-permute-start | bytes 1228808 | tf_op jit(solution)/shard_map/ppermute | solution.py:404
  617.2 31.9 %collective-permute-start.34 = (bf16[160,1280]{1,0:T(8,128)(2,1)}, bf16[160,1280]{1,0:T(8,128)(2,1)}, u32[]{:S(2)}, u32[]{:S(2)}) collective-permute-start(bf16[160,1280]{1,0:T(8,128)(2,1)} %copy.51), channel_id=1, source_target_pairs={{1,0},{2,3},{5,4},{6,7},{9,8},{10,11},{13,12},{14,15},{17,16},{18,... | collective-permute-start | bytes 1228808 | tf_op jit(solution)/shard_map/ppermute | solution.py:404
  (27 other events, 193.4 us)
Sparse Core Ops, SparseCore 0:
  78.2 33.1 all-gather.3
  113.2 32.8 all-gather.5
  148.0 37.0 all-gather.7
  254.3 95.1 reduce-scatter.3
